TPU v7x, 32 devices: a whole 2x2x4 slice. The times are simulated.
32 devices in a mesh: seq: 8 (over y, x, core), head: 4 (over z).
Axes of the slice: x: 2, y: 2, z: 4, core: 2. Of those that a mesh axis runs over, the one named last changes fastest.
Arguments:
- tokens: bfloat16 [65536, 512], P(('seq', 'head')), may hold values from -6 to 6
- seq_lengths: int32 [8, 16], P('seq'), may hold values from 0 to 1024, as said below
- ln1_gain: float32 [512], replicated, may hold values from 0.5 to 1.5
- ln1_bias: float32 [512], replicated, may hold values from -3 to 3
- w_qkv: bfloat16 [512, 1536], replicated, may hold values from -0.375 to 0.375
- w_out: bfloat16 [512, 512], replicated, may hold values from -1 to 1
- w_gate1: bfloat16 [512, 512], replicated, may hold values from -0.25 to 0.25
- gate1_gain: float32 [512], replicated, may hold values from 0.5 to 2
- gate1_shift: float32 [512], replicated, may hold values from -3 to 3
- ln2_gain: float32 [512], replicated, may hold values from 0.5 to 1.5
- ln2_bias: float32 [512], replicated, may hold values from -3 to 3
- w_up: bfloat16 [512, 2048], replicated, may hold values from -0.25 to 0.25
- b_up: float32 [2048], replicated, may hold values from -3 to 3
- w_down: bfloat16 [2048, 512], replicated, may hold values from -0.1875 to 0.1875
- b_down: float32 [512], replicated, may hold values from -3 to 3
- w_gate2: bfloat16 [512, 512], replicated, may hold values from -0.25 to 0.25
- gate2_gain: float32 [512], replicated, may hold values from 0.5 to 2
- gate2_shift: float32 [512], replicated, may hold values from -3 to 3
- cotangent: bfloat16 [65536, 512], P(('seq', 'head')), may hold values from -6 to 6
Outputs:
- output: bfloat16 [65536, 512], P(('seq', 'head'))
- grad_tokens: float32 [65536, 512], P(('seq', 'head'))
- g_ln1_gain: float32 [512], replicated
- g_ln1_bias: float32 [512], replicated
- g_w_qkv: float32 [512, 1536], replicated
- g_w_out: float32 [512, 512], replicated
- g_w_gate1: float32 [512, 512], replicated
- g_gate1_gain: float32 [512], replicated
- g_gate1_shift: float32 [512], replicated
- g_ln2_gain: float32 [512], replicated
- g_ln2_bias: float32 [512], replicated
- g_w_up: float32 [512, 2048], replicated
- g_b_up: float32 [2048], replicated
- g_w_down: float32 [2048, 512], replicated
- g_b_down: float32 [512], replicated
- g_w_gate2: float32 [512, 512], replicated
- g_gate2_gain: float32 [512], replicated
- g_gate2_shift: float32 [512], replicated
Inputs may be any that keep to these rules, and one draw needn't show every extreme that they name: `seq_lengths`: each row lists the lengths of its group's sequences in order, each 512 or 1024, the two lengths mixed in any order within a group, followed by zeros; each row sums to 8192.
All inputs are finite; a program needn't handle non-finite values.
Results may differ from a plain program's by a relative error of at most 0.013.
The roundings to bfloat16 on the way count: a program that leaves them out, or rounds other values in their place, can miss the bound.
Values may be sent and summed in bfloat16 or wider, within the bound.
No kernel may reach another device: no remote copies, remote signals or barrier semaphores. Data moves between devices by JAX's collectives and lax.ppermute only.
A program may use at most 256 MiB of HBM per device.

v0:
```python
import jax
import jax.numpy as jnp
from jax import lax
from jax.sharding import PartitionSpec as P

HEADS = 8
HD = 64
SHORT = 512


EPS = 1e-05
MASKED = -1e30


def shifted(x, axis, by):
    size = lax.axis_size(axis)
    pairs = [(i, i + by) for i in range(size) if 0 <= i + by < size]
    return lax.ppermute(x, axis, pairs)


def layer_norm(value, gain, shift):
    mean = jnp.mean(value, axis=-1, keepdims=True)
    centered = value - mean
    var = jnp.mean(centered * centered, axis=-1, keepdims=True)
    return centered * lax.rsqrt(var + EPS) * gain + shift


def continuation(lengths, span):
    starts = jnp.cumsum(lengths) - lengths
    begins = jnp.arange(lengths.shape[0], dtype=jnp.int32) * span
    hit = (starts[None, :] == begins[:, None]) & (lengths[None, :] > 0)
    return 1 - jnp.max(hit.astype(jnp.int32), axis=1)


def block_scores(q_block, k_block, scale):
    span = q_block.shape[0]
    width = k_block.shape[0]
    raw = jnp.einsum("qhd,khd->hqk", q_block, k_block, preferred_element_type=jnp.float32) * scale
    rows = lax.broadcasted_iota(jnp.int32, (span, width), 0)
    cols = lax.broadcasted_iota(jnp.int32, (span, width), 1)
    allowed = cols <= rows + (width - span)
    return jnp.where(allowed[None], raw, MASKED)


def block_forward(q_block, k_block, v_block, scale):
    scores = block_scores(q_block, k_block, scale)
    top = jnp.max(scores, axis=-1, keepdims=True)
    weights = jnp.exp(scores - top)
    total = jnp.sum(weights, axis=-1, keepdims=True)
    probs = (weights / total).astype(jnp.bfloat16)
    result = jnp.einsum("hqk,khd->qhd", probs, v_block, preferred_element_type=jnp.float32)
    return (result, (top + jnp.log(total))[..., 0])


def block_backward(q_block, k_block, v_block, grad_block, lse, scale):
    scores = block_scores(q_block, k_block, scale)
    probs = jnp.exp(scores - lse[..., None])
    dprobs = jnp.einsum("qhd,khd->hqk", grad_block, v_block, preferred_element_type=jnp.float32)
    delta = jnp.sum(probs * dprobs, axis=-1, keepdims=True)
    dscores = (probs * (dprobs - delta)).astype(jnp.bfloat16)
    grad_q = (
        jnp.einsum("hqk,khd->qhd", dscores, k_block, preferred_element_type=jnp.float32) * scale
    )
    grad_k = (
        jnp.einsum("hqk,qhd->khd", dscores, q_block, preferred_element_type=jnp.float32) * scale
    )
    grad_v = jnp.einsum(
        "hqk,qhd->khd", probs.astype(jnp.bfloat16), grad_block, preferred_element_type=jnp.float32
    )
    return (grad_q, grad_k, grad_v)


def attend(query, key_ext, value_ext, flags, span, scale):
    count = query.shape[0] // span

    def one_block(index):
        q_block = lax.dynamic_slice_in_dim(query, index * span, span, 0)
        k_block = lax.dynamic_slice_in_dim(key_ext, index * span, 2 * span, 0)
        v_block = lax.dynamic_slice_in_dim(value_ext, index * span, 2 * span, 0)

        def wide(unused):
            return block_forward(q_block, k_block, v_block, scale)

        def narrow(unused):
            return block_forward(q_block, k_block[span:], v_block[span:], scale)

        return lax.cond(flags[index] > 0, wide, narrow, 0)

    results, lses = lax.map(one_block, jnp.arange(count, dtype=jnp.int32))
    return (results.reshape(query.shape), lses)


def attend_back(query, key_ext, value_ext, grad, lses, flags, span, scale):
    count = query.shape[0] // span

    def one_block(index):
        q_block = lax.dynamic_slice_in_dim(query, index * span, span, 0)
        k_block = lax.dynamic_slice_in_dim(key_ext, index * span, 2 * span, 0)
        v_block = lax.dynamic_slice_in_dim(value_ext, index * span, 2 * span, 0)
        g_block = lax.dynamic_slice_in_dim(grad, index * span, span, 0)
        lse = lses[index]

        def wide(unused):
            grad_q, grad_k, grad_v = block_backward(q_block, k_block, v_block, g_block, lse, scale)
            return (grad_q, grad_k[:span], grad_k[span:], grad_v[:span], grad_v[span:])

        def narrow(unused):
            grad_q, grad_k, grad_v = block_backward(
                q_block, k_block[span:], v_block[span:], g_block, lse, scale
            )
            zeros = jnp.zeros_like(grad_k)
            return (grad_q, zeros, grad_k, zeros, grad_v)

        return lax.cond(flags[index] > 0, wide, narrow, 0)

    grad_q, kprev, kown, vprev, vown = lax.map(one_block, jnp.arange(count, dtype=jnp.int32))
    grad_k = kown + jnp.concatenate([kprev[1:], jnp.zeros_like(kprev[:1])], axis=0)
    grad_v = vown + jnp.concatenate([vprev[1:], jnp.zeros_like(vprev[:1])], axis=0)
    return (
        grad_q.reshape(query.shape),
        grad_k.reshape(query.shape),
        grad_v.reshape(query.shape),
        kprev[0],
        vprev[0],
    )


def gate_forward(logits, gain, shift, count):
    mean = lax.psum(jnp.sum(logits, axis=0), ("seq", "head")) / count
    centered = logits - mean
    var = lax.psum(jnp.sum(centered * centered, axis=0), ("seq", "head")) / count
    rstd = lax.rsqrt(var + EPS)
    normed = centered * rstd
    return (jax.nn.sigmoid(normed * gain + shift), normed, rstd)


def gate_backward(gate, normed, rstd, grad_gate, gain, count):
    grad_pre = grad_gate * gate * (1.0 - gate)
    shift_sum, gain_sum = lax.psum(
        (jnp.sum(grad_pre, axis=0), jnp.sum(grad_pre * normed, axis=0)), ("seq", "head")
    )
    grad_logits = gain * rstd * (grad_pre - shift_sum / count - normed * gain_sum / count)
    return (grad_logits.astype(jnp.bfloat16), gain_sum, shift_sum)


def tdot(left, right):
    return lax.dot_general(
        left, right, (((0,), (0,)), ((), ())), preferred_element_type=jnp.float32
    )


def body(
    tokens,
    seq_lengths,
    ln1_gain,
    ln1_bias,
    w_qkv,
    w_out,
    w_gate1,
    gate1_gain,
    gate1_shift,
    ln2_gain,
    ln2_bias,
    w_up,
    b_up,
    w_down,
    b_down,
    w_gate2,
    gate2_gain,
    gate2_shift,
    cotangent,
):
    rows, width = tokens.shape
    span = SHORT
    scale = HD ** (-0.5)
    count = rows * lax.axis_size("seq") * lax.axis_size("head")
    group_flags = continuation(seq_lengths[0], span)
    x = tokens.astype(jnp.float32)
    normed_one, ln1_pull = jax.vjp(layer_norm, x, ln1_gain, ln1_bias)
    h1 = normed_one.astype(jnp.bfloat16)
    qkv = jnp.dot(h1, w_qkv, preferred_element_type=jnp.float32).astype(jnp.bfloat16)
    query = qkv[:, :width]
    keys = qkv[:, width : 2 * width]
    values = qkv[:, 2 * width :]
    per_dev = rows // span
    local_flags = lax.dynamic_slice_in_dim(
        group_flags, lax.axis_index("head") * per_dev, per_dev, 0
    )
    tails = jnp.stack([keys[rows - span :], values[rows - span :]])
    before = shifted(tails, "head", 1)
    q_heads = query.reshape(rows, HEADS, HD)
    k_ext = jnp.concatenate([before[0], keys], axis=0).reshape(rows + span, HEADS, HD)
    v_ext = jnp.concatenate([before[1], values], axis=0).reshape(rows + span, HEADS, HD)
    result, lses = attend(q_heads, k_ext, v_ext, local_flags, span, scale)
    attended = result.reshape(rows, width).astype(jnp.bfloat16)
    branch = jnp.dot(attended, w_out, preferred_element_type=jnp.float32)
    z_one = jnp.dot(h1, w_gate1, preferred_element_type=jnp.float32)
    gate_one, nhat_one, rstd_one = gate_forward(z_one, gate1_gain, gate1_shift, count)
    mixed = gate_one * branch + (1.0 - gate_one) * x
    normed_two, ln2_pull = jax.vjp(layer_norm, mixed, ln2_gain, ln2_bias)
    h2 = normed_two.astype(jnp.bfloat16)
    pre = jnp.dot(h2, w_up, preferred_element_type=jnp.float32) + b_up
    act, gelu_pull = jax.vjp(jax.nn.gelu, pre)
    act_low = act.astype(jnp.bfloat16)
    mlp = jnp.dot(act_low, w_down, preferred_element_type=jnp.float32) + b_down
    z_two = jnp.dot(h2, w_gate2, preferred_element_type=jnp.float32)
    gate_two, nhat_two, rstd_two = gate_forward(z_two, gate2_gain, gate2_shift, count)
    output = (gate_two * mlp + (1.0 - gate_two) * mixed).astype(jnp.bfloat16)
    grad_out = cotangent.astype(jnp.float32)
    grad_mlp = (grad_out * gate_two).astype(jnp.bfloat16)
    grad_z_two, g_gate2_gain, g_gate2_shift = gate_backward(
        gate_two, nhat_two, rstd_two, grad_out * (mlp - mixed), gate2_gain, count
    )
    g_b_down = jnp.sum(grad_mlp.astype(jnp.float32), axis=0)
    g_w_down = tdot(act_low, grad_mlp)
    (grad_pre,) = gelu_pull(jnp.dot(grad_mlp, w_down.T, preferred_element_type=jnp.float32))
    grad_pre_low = grad_pre.astype(jnp.bfloat16)
    g_b_up = jnp.sum(grad_pre_low.astype(jnp.float32), axis=0)
    g_w_up = tdot(h2, grad_pre_low)
    g_w_gate2 = tdot(h2, grad_z_two)
    grad_h2 = jnp.dot(grad_pre_low, w_up.T, preferred_element_type=jnp.float32) + jnp.dot(
        grad_z_two, w_gate2.T, preferred_element_type=jnp.float32
    )
    grad_norm_two, g_ln2_gain, g_ln2_bias = ln2_pull(grad_h2)
    grad_mixed = grad_out * (1.0 - gate_two) + grad_norm_two
    grad_branch = (grad_mixed * gate_one).astype(jnp.bfloat16)
    grad_z_one, g_gate1_gain, g_gate1_shift = gate_backward(
        gate_one, nhat_one, rstd_one, grad_mixed * (branch - x), gate1_gain, count
    )
    grad_x = grad_mixed * (1.0 - gate_one)
    g_w_out = tdot(attended, grad_branch)
    grad_attended = jnp.dot(grad_branch, w_out.T, preferred_element_type=jnp.float32).astype(
        jnp.bfloat16
    )
    grad_q, grad_k, grad_v, kprev, vprev = attend_back(
        q_heads,
        k_ext,
        v_ext,
        grad_attended.reshape(rows, HEADS, HD),
        lses,
        local_flags,
        span,
        scale,
    )
    terms = jnp.stack([kprev.reshape(span, width), vprev.reshape(span, width)])
    arrived = shifted(terms.astype(jnp.bfloat16), "head", -1).astype(terms.dtype)
    grad_k = grad_k.reshape(rows, width)
    grad_v = grad_v.reshape(rows, width)
    grad_k = jnp.concatenate([grad_k[: rows - span], grad_k[rows - span :] + arrived[0]], axis=0)
    grad_v = jnp.concatenate([grad_v[: rows - span], grad_v[rows - span :] + arrived[1]], axis=0)
    grad_query = grad_q.reshape(rows, width).astype(jnp.bfloat16)
    grad_keys = grad_k.astype(jnp.bfloat16)
    grad_values = grad_v.astype(jnp.bfloat16)
    grad_qkv = jnp.concatenate([grad_query, grad_keys, grad_values], axis=1)
    g_w_qkv = tdot(h1, grad_qkv)
    g_w_gate1 = tdot(h1, grad_z_one)
    grad_h1 = jnp.dot(grad_qkv, w_qkv.T, preferred_element_type=jnp.float32) + jnp.dot(
        grad_z_one, w_gate1.T, preferred_element_type=jnp.float32
    )
    grad_norm_one, g_ln1_gain, g_ln1_bias = ln1_pull(grad_h1)
    grad_x = grad_x + grad_norm_one
    summed = lax.psum(
        (
            g_ln1_gain,
            g_ln1_bias,
            g_w_qkv,
            g_w_out,
            g_w_gate1,
            g_w_up,
            g_b_up,
            g_w_down,
            g_b_down,
            g_w_gate2,
            g_ln2_gain,
            g_ln2_bias,
        ),
        ("seq", "head"),
    )
    early = summed[:5]
    late = summed[5:]
    return (
        output,
        grad_x,
        early[0],
        early[1],
        early[2],
        early[3],
        early[4],
        g_gate1_gain,
        g_gate1_shift,
        late[5],
        late[6],
        late[0],
        late[1],
        late[2],
        late[3],
        late[4],
        g_gate2_gain,
        g_gate2_shift,
    )


def solution(mesh):
    return jax.shard_map(
        body,
        mesh=mesh,
        in_specs=(
            P(("seq", "head"), None),
            P("seq", None),
            P(),
            P(),
            P(),
            P(),
            P(),
            P(),
            P(),
            P(),
            P(),
            P(),
            P(),
            P(),
            P(),
            P(),
            P(),
            P(),
            P(("seq", "head"), None),
        ),
        out_specs=(
            P(("seq", "head"), None),
            P(("seq", "head"), None),
            P(),
            P(),
            P(),
            P(),
            P(),
            P(),
            P(),
            P(),
            P(),
            P(),
            P(),
            P(),
            P(),
            P(),
            P(),
            P(),
        ),
        check_vma=False,
    )
```

profile of v0, /device:TPU:0, one launch (start us, length us, event | category | flops | bytes accessed | tf_op | source)
XLA Modules:
  0.0 985.4 jit_solution(10945673425898489861)
XLA Ops:
  33.2 40.4 %psum.140 = f32[512]{0:T(512)S(1)} all-reduce(f32[512]{0:T(512)S(1)} %get-tuple-element.319), channel_id=1, replica_groups=mesh['seq'=8,'head'=4] {'seq','head'}, use_global_device_ids=true, to_apply=%region_3.4 | all-reduce | flops 512 | bytes 4096 | tf_op jit(solution)/shard_map/psum | solution.py:129
  76.5 38.9 %psum.141 = f32[512]{0:T(512)S(1)} all-reduce(f32[512]{0:T(512)S(1)} %multiply_reduce_fusion.8), channel_id=1, replica_groups=mesh['seq'=8,'head'=4] {'seq','head'}, use_global_device_ids=true, to_apply=%region_5.6 | all-reduce | flops 512 | bytes 4096 | tf_op jit(solution)/shard_map/psum | solution.py:131
  123.9 72.8 %while.30 = (s32[]{:T(128)}, bf16[4,512,8,64]{1,3,2,0:T(8,128)(2,1)}, f32[4,8,512]{2,1,0:T(8,128)}, s32[4]{0:T(128)S(1)}, s32[4]{0:T(128)S(1)}, /*index=5*/bf16[...) while((s32[]{:T(128)}, ...), condition=%wide.region_15.16_spmd, body=%wide.region_8.0_spmd.sunk | while | flops 1124594176 | bytes 62034292 | solution.py:89
  146.0 12.8 %conditional.4 = (bf16[1,512,8,64]{1,3,2,0:T(8,128)(2,1)S(1)}, f32[1,8,512]{2,1,0:T(8,128)S(1)}) conditional(s32[]{:T(128)} %bitcast.152, (bf16[1024,8,64]{0,2,1:T(8,128)(2,1)S(1)}, bf16[512,8,64]{0,2,1:T(8,128)(2,1)S(1)}, bf16[1024,8,64]{0,2,1:T(8,128)(2,1)S(1)}) %tuple.115, (bf16[512,8,64]{0,2,1:T(8,128)(2,1)S(1)}, ...), branch_computations={%region_9.11_spmd, %region_12.14_spmd} | conditional | flops 1124594176 | bytes 55709712 | solution.py:87
  182.3 12.8 %conditional.4 = (bf16[1,512,8,64]{1,3,2,0:T(8,128)(2,1)S(1)}, f32[1,8,512]{2,1,0:T(8,128)S(1)}) conditional(s32[]{:T(128)} %bitcast.152, (bf16[1024,8,64]{0,2,1:T(8,128)(2,1)S(1)}, bf16[512,8,64]{0,2,1:T(8,128)(2,1)S(1)}, bf16[1024,8,64]{0,2,1:T(8,128)(2,1)S(1)}) %tuple.115, (bf16[512,8,64]{0,2,1:T(8,128)(2,1)S(1)}, ...), branch_computations={%region_9.11_spmd, %region_12.14_spmd} | conditional | flops 1124594176 | bytes 55709712 | solution.py:87
  213.5 39.4 %psum.142 = f32[512]{0:T(512)S(1)} all-reduce(f32[512]{0:T(512)S(1)} %get-tuple-element.322), channel_id=1, replica_groups=mesh['seq'=8,'head'=4] {'seq','head'}, use_global_device_ids=true, to_apply=%region_19.20 | all-reduce | flops 512 | bytes 4096 | tf_op jit(solution)/shard_map/psum | solution.py:129
  255.6 40.6 %psum.143 = f32[512]{0:T(512)S(1)} all-reduce(f32[512]{0:T(512)S(1)} %multiply_reduce_fusion.6), channel_id=1, replica_groups=mesh['seq'=8,'head'=4] {'seq','head'}, use_global_device_ids=true, to_apply=%region_21.22 | all-reduce | flops 512 | bytes 4096 | tf_op jit(solution)/shard_map/psum | solution.py:131
  296.3 12.6 %multiply_convert_fusion.2 = (bf16[2048,2048]{1,0:T(8,128)(2,1)S(1)}, f32[2048,2048]{1,0:T(8,128)}) fusion(f32[2048]{0:T(1024)S(1)} %copy-done.82, bf16[2048,512]{1,0:T(8,128)(2,1)} %copy-done.21, bf16[512,2048]{1,0:T(8,128)(2,1)S(1)} %copy-done), kind=kOutput, calls=%fused_computation.85 | convolution fusion | flops 4336910336 | bytes 29368320 | tf_op jit(solution)/shard_map/dot_general | solution.py:202
  308.9 10.2 %fusion.82 = (f32[512]{0:T(512)S(1)}, f32[512]{0:T(512)S(1)}, f32[2048,512]{1,0:T(8,128)}, bf16[2048,512]{1,0:T(8,128)(2,1)}, f32[512]{0:T(512)}, /*index=5*/bf16[2048,512]{1,0:T(8,128)(2,1)}) fusion(f32[512]{0:T(512)S(1)} %get-tuple-element.318, f32[2048,512]{1,0:T(8,128)S(1)} %copy-done.3, f32[512]{0:T(512)S(1)} %broadcast_multiply_fusion.4, ...), kind=kOutput, calls=%fused_computation.185 | convolution fusion | flops 4321180160 | bytes 29376512 | tf_op jit(solution)/shard_map/dot_general | solution.py:205
  326.9 20.5 %convert_reduce_fusion = (f32[2048]{0:T(1024)}, bf16[2048,2048]{1,0:T(8,128)(2,1)}) fusion(f32[2048,2048]{1,0:T(8,128)} %get-tuple-element.325, f32[2048]{0:T(1024)S(1)} %copy-done.82, bf16[2048,512]{1,0:T(8,128)(2,1)} %get-tuple-element.301, bf16[2048,512]{1,0:T(8,128)(2,1)S(1)} %copy-done.79), kind=kOutput, calls=%fused_computation.84 | convolution fusion | flops 4391434240 | bytes 29376512 | tf_op jit(solution)/shard_map/dot_general | solution.py:216
  347.4 40.0 %all-reduce.4 = (f32[512]{0:T(512)S(1)}, f32[512]{0:T(512)S(1)}) all-reduce(f32[512]{0:T(512)S(1)} %get-tuple-element.211, f32[512]{0:T(512)S(1)} %get-tuple-element.210), channel_id=1, replica_groups=mesh['seq'=8,'head'=4] {'seq','head'}, use_global_device_ids=true, to_apply=%region_25.26 | all-reduce | flops 1024 | bytes 8192 | tf_op jit(solution)/shard_map/psum | solution.py:139
  413.7 40.1 %all-reduce.3 = (f32[512]{0:T(512)S(1)}, f32[512]{0:T(512)S(1)}) all-reduce(f32[512]{0:T(512)S(1)} %get-tuple-element.209, f32[512]{0:T(512)S(1)} %get-tuple-element.208), channel_id=1, replica_groups=mesh['seq'=8,'head'=4] {'seq','head'}, use_global_device_ids=true, to_apply=%region_37.38 | all-reduce | flops 1024 | bytes 8192 | tf_op jit(solution)/shard_map/psum | solution.py:139
  474.3 179.7 %while.31 = (s32[]{:T(128)}, bf16[4,512,8,64]{1,3,2,0:T(8,128)(2,1)}, f32[4,512,8,64]{1,3,2,0:T(8,128)}, f32[4,512,8,64]{1,3,2,0:T(8,128)}, f32[4,512,8,64]{1,3,...) while((s32[]{:T(128)}, ...), condition=%wide.region_33.34_spmd, body=%wide.region_28.33_spmd.sunk | while | flops 2723672576 | bytes 213537392 | solution.py:116
  484.7 15.5 %conditional.5 = (bf16[1,512,8,64]{1,3,2,0:T(8,128)(2,1)S(1)}, f32[1,512,8,64]{1,3,2,0:T(8,128)}, f32[1,512,8,64]{1,3,2,0:T(8,128)S(1)}, f32[1,512,8,64]{1,3,2,0:T(8,128)}, f32[1,512,8,64]{1,3,2,0:T(8,128)S(1)}) conditional(s32[]{:T(128)} %bitcast.154, (bf16[1024,8,64]{0,2,1:T(8,128)(2,1)}, bf16[512,8,64]{0,2,1:T(8,128)(2,1)S(1)}, ...), branch_computations={%region_29.30_spmd, %region_31.32_spmd} | conditional | flops 2723672576 | bytes 180998272 | solution.py:114
  516.6 41.1 %conditional.5 = (bf16[1,512,8,64]{1,3,2,0:T(8,128)(2,1)S(1)}, f32[1,512,8,64]{1,3,2,0:T(8,128)}, f32[1,512,8,64]{1,3,2,0:T(8,128)S(1)}, f32[1,512,8,64]{1,3,2,0:T(8,128)}, f32[1,512,8,64]{1,3,2,0:T(8,128)S(1)}) conditional(s32[]{:T(128)} %bitcast.154, (bf16[1024,8,64]{0,2,1:T(8,128)(2,1)}, bf16[512,8,64]{0,2,1:T(8,128)(2,1)S(1)}, ...), branch_computations={%region_29.30_spmd, %region_31.32_spmd} | conditional | flops 2723672576 | bytes 180998272 | solution.py:114
  520.8 11.2 %multiply_reduce_fusion.1 = (f32[8,512]{1,0:T(8,128)}, f32[8,512,1024]{2,1,0:T(8,128)}) fusion(f32[8,512,1024]{2,1,0:T(8,128)S(1)} %fusion.95, f32[8,512]{1,0:T(8,128)} %bitcast.165, bf16[512,8,64]{0,2,1:T(8,128)(2,1)S(1)} %get-tuple-element.145, bf16[1024,8,64]{0,2,1:T(8,128)(2,1)} %get-tuple-element.146, pred[512,1024]{1,0:T(8,128)(4,1)} %iota_compare_fusion.3), kind=kOutput, calls=%fused_computation.51 | convolution fusion | flops 557838336 | bytes 35684352 | tf_op jit(solution)/shard_map/while/body/eval_jaxpr/cond/branch_1_fun/qhd,khd->hqk/dot_general | solution.py:38
  532.1 9.3 multiply_convert_fusion.1
  574.3 15.5 %conditional.5 = (bf16[1,512,8,64]{1,3,2,0:T(8,128)(2,1)S(1)}, f32[1,512,8,64]{1,3,2,0:T(8,128)}, f32[1,512,8,64]{1,3,2,0:T(8,128)S(1)}, f32[1,512,8,64]{1,3,2,0:T(8,128)}, f32[1,512,8,64]{1,3,2,0:T(8,128)S(1)}) conditional(s32[]{:T(128)} %bitcast.154, (bf16[1024,8,64]{0,2,1:T(8,128)(2,1)}, bf16[512,8,64]{0,2,1:T(8,128)(2,1)S(1)}, ...), branch_computations={%region_29.30_spmd, %region_31.32_spmd} | conditional | flops 2723672576 | bytes 180998272 | solution.py:114
  606.2 41.1 %conditional.5 = (bf16[1,512,8,64]{1,3,2,0:T(8,128)(2,1)S(1)}, f32[1,512,8,64]{1,3,2,0:T(8,128)}, f32[1,512,8,64]{1,3,2,0:T(8,128)S(1)}, f32[1,512,8,64]{1,3,2,0:T(8,128)}, f32[1,512,8,64]{1,3,2,0:T(8,128)S(1)}) conditional(s32[]{:T(128)} %bitcast.154, (bf16[1024,8,64]{0,2,1:T(8,128)(2,1)}, bf16[512,8,64]{0,2,1:T(8,128)(2,1)S(1)}, ...), branch_computations={%region_29.30_spmd, %region_31.32_spmd} | conditional | flops 2723672576 | bytes 180998272 | solution.py:114
  610.4 11.2 %multiply_reduce_fusion.1 = (f32[8,512]{1,0:T(8,128)}, f32[8,512,1024]{2,1,0:T(8,128)}) fusion(f32[8,512,1024]{2,1,0:T(8,128)S(1)} %fusion.95, f32[8,512]{1,0:T(8,128)} %bitcast.165, bf16[512,8,64]{0,2,1:T(8,128)(2,1)S(1)} %get-tuple-element.145, bf16[1024,8,64]{0,2,1:T(8,128)(2,1)} %get-tuple-element.146, pred[512,1024]{1,0:T(8,128)(4,1)} %iota_compare_fusion.3), kind=kOutput, calls=%fused_computation.51 | convolution fusion | flops 557838336 | bytes 35684352 | tf_op jit(solution)/shard_map/while/body/eval_jaxpr/cond/branch_1_fun/qhd,khd->hqk/dot_general | solution.py:38
  687.0 14.5 %collective-permute-done.1 = bf16[2,512,512]{1,2,0:T(8,128)(2,1)S(1)} collective-permute-done((bf16[2,512,512]{1,2,0:T(8,128)(2,1)S(1)}, bf16[2,512,512]{1,2,0:T(8,128)(2,1)S(1)}, u32[]{:S(2)}, u32[]{:S(2)}) %collective-permute-start.1) | collective-permute-done | bytes 1048608 | tf_op jit(solution)/shard_map/ppermute | solution.py:18
  708.2 12.8 %fusion.72 = f32[2048,512]{1,0:T(8,128)S(1)} fusion(bf16[512,1536]{1,0:T(8,128)(2,1)} %param.31, bf16[512,512]{0,1:T(8,128)(2,1)S(1)} %get-tuple-element.312, bf16[1536,512]{0,1:T(8,128)(2,1)} %bitcast.176, bf16[512,512]{0,1:T(8,128)(2,1)S(1)} %get-tuple-element.311, bf16[1536,512]{0,1:T(8,128)(2,1)} %bitcast.178, bf16[2048,512]{0,1:T(8,128)(2,1)} %bitcast.170), kind=kOutput, calls=%fused_computation.179 | convolution fusion | flops 3252682752 | bytes 12058624 | tf_op jit(solution)/shard_map/dot_general | solution.py:257
  727.1 41.0 %all-reduce.2 = (f32[512]{0:T(512)}, f32[512]{0:T(512)}, f32[512]{0:T(512)}, f32[512]{0:T(512)}, f32[2048]{0:T(1024)}, /*index=5*/f32[512]{0:T(512)}) all-reduce(f32[512]{0:T(512)S(1)} %get-tuple-element.203, f32[512]{0:T(512)S(1)} %get-tuple-element.206, f32[512]{0:T(512)S(1)} %copy-done.67, ...), channel_id=1, replica_groups=mesh['seq'=8,'head'=4] {'seq','head'}, use_global_device_ids=true, to_apply=%region_41.42 | all-reduce | flops 4608 | bytes 36864 | tf_op jit(solution)/shard_map/psum | solution.py:262
  776.8 188.9 %all-reduce.8.cloned.1.call-done = (f32[512,1536]{1,0:T(8,128)}, f32[512,512]{1,0:T(8,128)}, f32[512,512]{1,0:T(8,128)}, f32[512,2048]{1,0:T(8,128)}, f32[2048,512]{1,0:T(8,128)}, /*index=5*/f32[512,512]{1,0:T(8,128)}) async-done(((f32[512,1536]{1,0:T(8,128)}, f32[512,512]{1,0:T(8,128)}, f32[512,512]{1,0:T(8,128)}, f32[512,2048]{1,0:T(8,128)}, f32[2048,512]{1,0:T(8,128)}, /*index=5*/f32[512,512]{1,0:T(8,128)}), ...) | async-done | bytes 14680080 | tf_op jit(solution)/shard_map/psum | solution.py:262
  (419 shorter events, 382.2 us)
Async XLA Ops:
  7.2 289.0 %copy-start = (bf16[512,2048]{1,0:T(8,128)(2,1)S(1)}, bf16[512,2048]{1,0:T(8,128)(2,1)}, u32[]{:S(2)}) copy-start(bf16[512,2048]{1,0:T(8,128)(2,1)} %param.38) | copy-start | bytes 6291460
  7.2 958.5 %all-reduce.8.cloned.1.call-start = ((), (), s32[]{:S(2)}) async-start(), calls=%async_computation | async-start | bytes 29360128 | tf_op jit(solution)/shard_map/psum | solution.py:262
  9.4 20.9 %copy-start.48 = (f32[2048]{0:T(1024)}, f32[2048]{0:T(1024)S(1)}, u32[]{:S(2)}) copy-start(f32[2048]{0:T(1024)S(1)} %broadcast_multiply_fusion.1) | copy-start | bytes 24580
  12.0 18.3 %copy-start.50 = (f32[2048]{0:T(1024)}, f32[2048]{0:T(1024)S(1)}, u32[]{:S(2)}) copy-start(f32[2048]{0:T(1024)S(1)} %fusion.67) | copy-start | bytes 24580
  20.0 101.3 %collective-permute-start = (bf16[2,512,512]{1,2,0:T(8,128)(2,1)}, bf16[2,512,512]{1,2,0:T(8,128)(2,1)S(1)}, u32[]{:S(2)}, u32[]{:S(2)}) collective-permute-start(bf16[2,512,512]{1,2,0:T(8,128)(2,1)} %pad_maximum_fusion.2), channel_id=1, source_target_pairs={{0,1},{1,2},{2,3},{4,5},{5,6},{6,7},{8,9},{9,10},{10,11},{12,13},{... | collective-permute-start | bytes 3145736 | tf_op jit(solution)/shard_map/ppermute | solution.py:18
  33.2 82.1 %copy-start.57 = (f32[512]{0:T(512)S(1)}, f32[512]{0:T(512)}, u32[]{:S(2)}) copy-start(f32[512]{0:T(512)} %param.34) | copy-start | bytes 6148
  73.7 47.6 %copy-start.54 = (f32[512]{0:T(512)}, f32[512]{0:T(512)S(1)}, u32[]{:S(2)}) copy-start(f32[512]{0:T(512)S(1)} %broadcast_multiply_fusion.5) | copy-start | bytes 6148
  213.5 82.7 %copy-start.69 = (f32[512]{0:T(512)S(1)}, f32[512]{0:T(512)}, u32[]{:S(2)}) copy-start(f32[512]{0:T(512)} %param.43) | copy-start | bytes 6148
  213.5 82.7 %copy-start.82 = (f32[2048]{0:T(1024)S(1)}, f32[2048]{0:T(1024)}, u32[]{:S(2)}) copy-start(f32[2048]{0:T(1024)} %param.39) | copy-start | bytes 24580
  296.2 12.7 %copy-start.3 = (f32[2048,512]{1,0:T(8,128)S(1)}, f32[2048,512]{1,0:T(8,128)}, u32[]{:S(2)}) copy-start(f32[2048,512]{1,0:T(8,128)} %get-tuple-element.323) | copy-start | bytes 12582916
  296.2 12.7 %copy-start.11 = (f32[2048,512]{1,0:T(8,128)S(1)}, f32[2048,512]{1,0:T(8,128)}, u32[]{:S(2)}) copy-start(f32[2048,512]{1,0:T(8,128)} %copy-done.10) | copy-start | bytes 12582916
  406.9 47.0 %copy-start.70 = (f32[512]{0:T(512)S(1)}, f32[512]{0:T(512)}, u32[]{:S(2)}) copy-start(f32[512]{0:T(512)} %get-tuple-element.315) | copy-start | bytes 6148
  674.8 27.6 %copy-start.41 = (bf16[64,8,3,512]{3,1,2,0:T(8,128)(2,1)}, bf16[64,8,3,512]{3,1,2,0:T(8,128)(2,1)S(1)}, u32[]{:S(2)}) copy-start(bf16[64,8,3,512]{3,1,2,0:T(8,128)(2,1)S(1)} %copy.66) | copy-start | bytes 4718596
  676.7 25.7 %copy-start.42 = (bf16[64,8,3,512]{3,1,2,0:T(8,128)(2,1)}, bf16[64,8,3,512]{3,1,2,0:T(8,128)(2,1)S(1)}, u32[]{:S(2)}) copy-start(bf16[64,8,3,512]{3,1,2,0:T(8,128)(2,1)S(1)} %copy.65) | copy-start | bytes 4718596
  676.8 24.7 %collective-permute-start.1 = (bf16[2,512,512]{1,2,0:T(8,128)(2,1)S(1)}, bf16[2,512,512]{1,2,0:T(8,128)(2,1)S(1)}, u32[]{:S(2)}, u32[]{:S(2)}) collective-permute-start(bf16[2,512,512]{1,2,0:T(8,128)(2,1)S(1)} %pad_maximum_fusion.3), channel_id=1, source_target_pairs={{1,0},{2,1},{3,2},{5,4},{6,5},{7,6},{9,8},{10,9},{11,10},{13,12},{... | collective-permute-start | bytes 3145736 | tf_op jit(solution)/shard_map/ppermute | solution.py:18
  680.7 21.7 %copy-start.38 = (bf16[64,8,4,512]{3,1,2,0:T(8,128)(2,1)}, bf16[64,8,4,512]{3,1,2,0:T(8,128)(2,1)S(1)}, u32[]{:S(2)}) copy-start(bf16[64,8,4,512]{3,1,2,0:T(8,128)(2,1)S(1)} %copy.64) | copy-start | bytes 6291460
  680.7 21.1 %slice-start = ((f32[4,512,8,64]{1,3,2,0:T(8,128)}), f32[1,512,8,64]{1,3,2,0:T(8,128)S(1)}, s32[]{:S(2)}) async-start(f32[4,512,8,64]{1,3,2,0:T(8,128)} %copy-done.24), calls=%async_computation.1 | async-start | bytes 2097152 | tf_op jit(solution)/shard_map/slice | solution.py:250
  680.7 21.1 %slice-start.1 = ((f32[4,512,8,64]{1,3,2,0:T(8,128)}), f32[1,512,8,64]{1,3,2,0:T(8,128)S(1)}, s32[]{:S(2)}) async-start(f32[4,512,8,64]{1,3,2,0:T(8,128)} %copy-done.25), calls=%async_computation.2 | async-start | bytes 2097152 | tf_op jit(solution)/shard_map/slice | solution.py:249
  708.2 12.8 %copy-start.28 = (bf16[2048,512]{1,0:T(8,128)(2,1)S(1)}, bf16[2048,512]{1,0:T(8,128)(2,1)}, u32[]{:S(2)}) copy-start(bf16[2048,512]{1,0:T(8,128)(2,1)} %get-tuple-element.307) | copy-start | bytes 6291460
  708.2 12.8 %copy-start.47 = (bf16[512,512]{1,0:T(8,128)(2,1)S(1)}, bf16[512,512]{1,0:T(8,128)(2,1)}, u32[]{:S(2)}) copy-start(bf16[512,512]{1,0:T(8,128)(2,1)} %param.33) | copy-start | bytes 1572868
  723.1 45.0 %copy-start.56 = (f32[512]{0:T(512)S(1)}, f32[512]{0:T(512)}, u32[]{:S(2)}) copy-start(f32[512]{0:T(512)} %copy-done.54) | copy-start | bytes 6148
  723.1 45.0 %copy-start.59 = (f32[512]{0:T(512)S(1)}, f32[512]{0:T(512)}, u32[]{:S(2)}) copy-start(f32[512]{0:T(512)} %param.34) | copy-start | bytes 6148
  723.1 45.0 %copy-start.61 = (f32[512]{0:T(512)S(1)}, f32[512]{0:T(512)}, u32[]{:S(2)}) copy-start(f32[512]{0:T(512)} %get-tuple-element.316) | copy-start | bytes 6148
  723.1 45.0 %copy-start.63 = (f32[512]{0:T(512)S(1)}, f32[512]{0:T(512)}, u32[]{:S(2)}) copy-start(f32[512]{0:T(512)} %param.35) | copy-start | bytes 6148
  (82 other events, 395.6 us)
Sparse Core Ops, SparseCore 0:
  708.3 257.3 all-reduce.7
where the time goes:
time: 995 us; the launch traced here: 985 us
  blocking collectives  280 us (28%)
  matrix products  211 us (21%)
  waiting for transfers between devices  203 us (20%)
  local copies, waits for them, and re-layouts  149 us (15%)
  other arithmetic  91.5 us (9%)
  loops' own time  27.5 us (3%)
  between operations  15.5 us (2%)
    psum x1, waiting for transfers between devices, body(): lax.psum((g_ln1_gain, g_ln1_bias, g_w_qkv, g_w_out, g_w_gate1, g_w_up, g_...  189 us
    psum x2, blocking collectives, gate_backward(): lax.psum((jnp.sum(grad_pre, axis=0), jnp.sum(grad_pre * normed, axis=0)),...  80.1 us
    psum x2, blocking collectives, gate_forward(): mean = lax.psum(jnp.sum(logits, axis=0), ('seq', 'head')) / count  79.8 us
    psum x2, blocking collectives, gate_forward(): lax.psum(jnp.sum(centered * centered, axis=0), ('seq', 'head')) / count  79.5 us
    psum x1, blocking collectives, body(): lax.psum((g_ln1_gain, g_ln1_bias, g_w_qkv, g_w_out, g_w_gate1, g_w_up, g_...  41 us
    dot_general x8, matrix products, block_scores(): jnp.einsum('qhd,khd->hqk', q_block, k_block, preferred_element_type=jnp.f...  36.2 us
    unnamed x185, local copies, waits for them, and re-layouts  35.5 us
    dynamic_update_slice x20, local copies, waits for them, and re-layouts, attend(): results, lses = lax.map(one_block, jnp.arange(count, dtype=jnp.int32))  31.8 us
  transfers between devices with their start and end apart: 3, of which 2 were waited for; matrix products, arithmetic and copies ran while one was open for 5% of the time, Pallas kernels for 0%

commit v1 on v0

v1 whole, which is shorter than its diff:
```python
import functools

import jax
import jax.numpy as jnp
from jax import lax
from jax.experimental import pallas as pl
from jax.experimental.pallas import tpu as pltpu
from jax.sharding import PartitionSpec as P

HD = 64
SPAN = 512
HALF = 256
PAIR = 128
EPS = 1e-05
MASKED = -1e30
SCALE = 0.125
AXES = ("seq", "head")
MIB = 1024 * 1024

F32 = jnp.float32
BF16 = jnp.bfloat16


def dot(a, b):
    return jnp.dot(a, b, preferred_element_type=F32)


def dot_nt(a, b):
    return lax.dot_general(a, b, (((1,), (1,)), ((), ())), preferred_element_type=F32)


def dot_tn(a, b):
    return lax.dot_general(a, b, (((0,), (0,)), ((), ())), preferred_element_type=F32)


def struct(shape, dtype):
    return jax.ShapeDtypeStruct(shape, dtype)


def params(mib, dims=1):
    return pltpu.CompilerParams(
        vmem_limit_bytes=mib * MIB, dimension_semantics=("arbitrary",) * dims
    )


def cost(flops, nbytes, trans=0):
    return pl.CostEstimate(flops=int(flops), bytes_accessed=int(nbytes), transcendentals=int(trans))


def rows_of(width, tile=SPAN):
    return pl.BlockSpec((tile, width), lambda i: (i, 0))


def whole(shape):
    return pl.BlockSpec(shape, lambda *_: (0,) * len(shape))


def normed(v):
    centered = v - jnp.mean(v, axis=-1, keepdims=True)
    rstd = lax.rsqrt(jnp.mean(centered * centered, axis=-1, keepdims=True) + EPS)
    return centered * rstd, rstd


def row(ref):
    return ref[...].reshape(1, -1)


def column_sum(v):
    return jnp.sum(v, axis=0, keepdims=True)


def add_stats(acc, z, i):
    n = z.shape[0]
    mean = column_sum(z) * (1.0 / n)
    c = z - mean
    dev = column_sum(c * c)

    @pl.when(i == 0)
    def _():
        acc[0:1, :] = mean
        acc[1:2, :] = dev

    @pl.when(i > 0)
    def _():
        before = i.astype(F32)
        gap = mean - acc[0:1, :]
        acc[0:1, :] += gap / (before + 1.0)
        acc[1:2, :] += dev + gap * gap * (n * before / (before + 1.0))


def add_sums(acc, sums, i):
    for j, s in enumerate(sums):

        @pl.when(i == 0)
        def _(j=j, s=s):
            acc[j : j + 1, :] = s

        @pl.when(i > 0)
        def _(j=j, s=s):
            acc[j : j + 1, :] += s


def spread(acc, out):
    out[...] = jnp.broadcast_to(acc[...][None], out.shape)


def merge_stats(parts, rows):
    n = parts.shape[0]
    means = parts[:, 0, :]
    mean = jnp.mean(means, axis=0, keepdims=True)
    gaps = means - mean
    dev = jnp.sum(parts[:, 1, :], axis=0, keepdims=True) + rows * jnp.sum(
        gaps * gaps, axis=0, keepdims=True
    )
    return mean, lax.rsqrt(dev * (1.0 / (rows * n)) + EPS)


def exchange(spread_rows):
    return lax.all_to_all(spread_rows, AXES, 0, 0, tiled=True)


def first_kernel(x, gain, bias, w_qkv, w_gate, h1, qkv, z1, stats, acc):
    i = pl.program_id(0)
    n, _ = normed(x[...].astype(F32))
    h = (n * row(gain) + row(bias)).astype(BF16)
    h1[...] = h
    qkv[...] = dot(h, w_qkv[...]).astype(BF16)
    z = dot(h, w_gate[...])
    z1[...] = z
    add_stats(acc, z, i)

    @pl.when(i == pl.num_programs(0) - 1)
    def _():
        spread(acc, stats)


def halo_kernel(x, gain, bias, w_qkv, kv):
    n, _ = normed(x[...].astype(F32))
    h = (n * row(gain) + row(bias)).astype(BF16)
    width = x.shape[1]
    kv[...] = dot(h, w_qkv[:, width:]).astype(BF16)


def diagonal():
    rows = lax.broadcasted_iota(jnp.int32, (HALF, HALF), 0)
    cols = lax.broadcasted_iota(jnp.int32, (HALF, HALF), 1)
    return rows, cols


def attend_kernel(flags, q, k, v, kp, vp, kh, vh, out, lse):
    b = pl.program_id(1)
    low = lax.broadcasted_iota(jnp.int32, (1, PAIR), 1) < HD

    def compute(wide):
        rows, cols = diagonal()
        allowed = cols <= rows
        if wide:
            first = b == 0
            k_prev = jnp.where(first, kh[...], kp[...])
            v_prev = jnp.where(first, vh[...], vp[...])
        for half in range(2):
            at = slice(half * HALF, (half + 1) * HALF)
            q_half = q[at, :] * jnp.asarray(SCALE, BF16)
            outs, tops = [], []
            for s in range(2):
                q_s = jnp.where(low if s == 0 else ~low, q_half, jnp.zeros_like(q_half))
                pieces = [(jnp.where(allowed, dot_nt(q_s, k[at, :]), MASKED), v[at, :])]
                if half:
                    pieces.append((dot_nt(q_s, k[:HALF, :]), v[:HALF, :]))
                if wide:
                    pieces.append((dot_nt(q_s, k_prev), v_prev))
                top = functools.reduce(
                    jnp.maximum, [jnp.max(p, axis=-1, keepdims=True) for p, _ in pieces]
                )
                total, acc = 0.0, 0.0
                for p, vals in pieces:
                    e = jnp.exp(p - top)
                    total = total + jnp.sum(e, axis=-1, keepdims=True)
                    acc = acc + dot(e.astype(BF16), vals)
                outs.append(acc / total)
                tops.append(top + jnp.log(total))
            out[at, :] = jnp.where(low, outs[0], outs[1]).astype(BF16)
            turned = jnp.where(low, tops[0], tops[1]).T
            lse[0, 0:1, at] = turned[0:1, :]
            lse[0, 1:2, at] = turned[HD : HD + 1, :]

    wide = flags[b] > 0
    pl.when(wide)(functools.partial(compute, True))
    pl.when(jnp.logical_not(wide))(functools.partial(compute, False))


def mix_kernel(
    rows, att, x, z1, parts, gain, shift, ln_gain, ln_bias, w_out, w_gate, y1, h2, z2, stats, acc, st
):
    i = pl.program_id(0)

    @pl.when(i == 0)
    def _():
        mean, rstd = merge_stats(parts, rows)
        st[0:1, :] = mean
        st[1:2, :] = rstd

    branch = dot(att[...], w_out[...])
    nhat = (z1[...] - st[0:1, :]) * st[1:2, :]
    t = jax.nn.sigmoid(nhat * row(gain) + row(shift))
    y = t * branch + (1.0 - t) * x[...].astype(F32)
    y1[...] = y
    n, _ = normed(y)
    h = (n * row(ln_gain) + row(ln_bias)).astype(BF16)
    h2[...] = h
    z = dot(h, w_gate[...])
    z2[...] = z
    add_stats(acc, z, i)

    @pl.when(i == pl.num_programs(0) - 1)
    def _():
        spread(acc, stats)


GELU_C = 0.7978845608028654
GELU_A = 0.044715


def mlp_kernel(h2, w_up, b_up, w_down, b_down, act, slope, mlp):
    h = h2[...]
    units = w_up.shape[1]
    total = row(b_down)
    step = 512
    bias = row(b_up)
    for j in range(units // step):
        at = slice(j * step, (j + 1) * step)
        pre = dot(h, w_up[:, at]) + bias[:, at]
        sq = pre * pre
        th = jnp.tanh(pre * (GELU_C + (GELU_C * GELU_A) * sq))
        cdf = 0.5 + 0.5 * th
        a = (pre * cdf).astype(BF16)
        g = cdf + pre * (0.5 - 0.5 * th * th) * (GELU_C + (3.0 * GELU_C * GELU_A) * sq)
        act[:, at] = a
        slope[:, at] = g.astype(BF16)
        total = total + dot(a, w_down[at, :])
    mlp[...] = total


def gate2_kernel(rows, mlp, y1, z2, c, parts, gain, shift, out, dmlp, sums, acc, st):
    i = pl.program_id(0)

    @pl.when(i == 0)
    def _():
        mean, rstd = merge_stats(parts, rows)
        st[0:1, :] = mean
        st[1:2, :] = rstd

    nhat = (z2[...] - st[0:1, :]) * st[1:2, :]
    t = jax.nn.sigmoid(nhat * row(gain) + row(shift))
    m, y = mlp[...], y1[...]
    out[...] = (t * m + (1.0 - t) * y).astype(BF16)
    g = c[...].astype(F32)
    dmlp[...] = (g * t).astype(BF16)
    du = g * (m - y) * t * (1.0 - t)
    add_sums(acc, [column_sum(du), column_sum(du * nhat)], i)

    @pl.when(i == pl.num_programs(0) - 1)
    def _():
        spread(acc, sums)


def mlp_back_kernel(dmlp, act, slope, h2, w_up, w_down, dh2, g_up, g_down, g_b, acc_up, acc_down):
    i = pl.program_id(0)

    @pl.when(i == 0)
    def _():
        acc_up[...] = jnp.zeros_like(acc_up)
        acc_down[...] = jnp.zeros_like(acc_down)
        g_b[...] = jnp.zeros_like(g_b)

    d, h = dmlp[...], h2[...]
    units = w_up.shape[1]
    step = 512
    total = 0.0
    width = d.shape[1]
    for j in range(units // step):
        at = slice(j * step, (j + 1) * step)
        dp = (dot_nt(d, w_down[at, :]) * slope[:, at].astype(F32)).astype(BF16)
        g_b[0:1, at] += column_sum(dp.astype(F32))
        total = total + dot_nt(dp, w_up[:, at])
        acc_up[:, at] += dot_tn(h, dp)
        acc_down[:, at] += dot_tn(d, act[:, at])
    dh2[...] = total
    g_b[1:2, 0:width] += column_sum(d.astype(F32))

    @pl.when(i == pl.num_programs(0) - 1)
    def _():
        g_up[...] = acc_up[...].astype(BF16)
        for j in range(units // step):
            at = slice(j * step, (j + 1) * step)
            g_down[at, :] = acc_down[:, at].T.astype(BF16)


def middle_kernel(
    rows,
    c,
    mlp,
    y1,
    z2,
    dh2p,
    att,
    x,
    z1,
    h2,
    parts2,
    sums2,
    parts1,
    gain2,
    shift2,
    gain1,
    shift1,
    ln_gain,
    w_gate2,
    w_out,
    gx,
    du1,
    datt,
    delta,
    g_w,
    sums,
    g_gate2,
    acc,
    st,
    acc_gate,
    acc_out,
):
    i = pl.program_id(0)
    count = 1.0 / (rows * parts2.shape[0])
    width = y1.shape[1]

    @pl.when(i == 0)
    def _():
        mean, rstd = merge_stats(parts2, rows)
        st[0:1, :] = mean
        st[1:2, :] = rstd
        mean, rstd = merge_stats(parts1, rows)
        st[2:3, :] = mean
        st[3:4, :] = rstd
        st[4:5, :] = jnp.sum(sums2[:, 0, :], axis=0, keepdims=True)
        st[5:6, :] = jnp.sum(sums2[:, 1, :], axis=0, keepdims=True)
        g_gate2[...] = st[4:6, :]
        acc_gate[...] = jnp.zeros_like(acc_gate)
        acc_out[...] = jnp.zeros_like(acc_out)

    g = c[...].astype(F32)
    y = y1[...]
    nhat2 = (z2[...] - st[0:1, :]) * st[1:2, :]
    t2 = jax.nn.sigmoid(nhat2 * row(gain2) + row(shift2))
    du2 = g * (mlp[...] - y) * t2 * (1.0 - t2)
    dz2 = (
        (row(gain2) * st[1:2, :]) * (du2 - st[4:5, :] * count - nhat2 * (st[5:6, :] * count))
    ).astype(BF16)
    acc_gate[...] += dot_tn(h2[...], dz2)
    dh2 = dh2p[...] + dot_nt(dz2, w_gate2[...])
    n, r = normed(y)
    e = dh2 * row(ln_gain)
    dy = g * (1.0 - t2) + r * (
        e - jnp.mean(e, axis=-1, keepdims=True) - n * jnp.mean(e * n, axis=-1, keepdims=True)
    )
    a = att[...]
    branch = dot(a, w_out[...])
    nhat1 = (z1[...] - st[2:3, :]) * st[3:4, :]
    t1 = jax.nn.sigmoid(nhat1 * row(gain1) + row(shift1))
    dbranch = (dy * t1).astype(BF16)
    gx[...] = dy * (1.0 - t1)
    du = dy * (branch - x[...].astype(F32)) * t1 * (1.0 - t1)
    du1[...] = du
    acc_out[...] += dot_tn(a, dbranch)
    da = dot_nt(dbranch, w_out[...]).astype(BF16)
    datt[...] = da
    prod = da.astype(F32) * a.astype(F32)
    hi = prod.astype(BF16)
    lo = (prod - hi.astype(F32)).astype(BF16)
    heads = width // HD
    pick = (
        lax.broadcasted_iota(jnp.int32, (heads, width), 1) // HD
        == lax.broadcasted_iota(jnp.int32, (heads, width), 0)
    ).astype(BF16)
    dl = dot_nt(pick, hi) + dot_nt(pick, lo)
    for p in range(heads // 2):
        delta[p] = dl[2 * p : 2 * p + 2, :]
    add_sums(
        acc, [column_sum(du), column_sum(du * nhat1), column_sum(dh2 * n), column_sum(dh2)], i
    )

    @pl.when(i == pl.num_programs(0) - 1)
    def _():
        spread(acc, sums)
        g_w[0:width, :] = acc_gate[...].astype(BF16)
        g_w[width:, :] = acc_out[...].astype(BF16)


def attend_back_unit(q_s, do_s, k_c, v_c, kt_s, lse, delta, mask):
    p = jnp.exp(dot_nt(k_c, q_s) - lse)
    if mask is not None:
        p = jnp.where(mask, p, 0.0)
    ds = (p * (dot_nt(v_c, do_s) - delta)).astype(BF16)
    return dot(ds, q_s), dot(p.astype(BF16), do_s), dot(kt_s, ds)


def head_inputs(q, do, s, low):
    pick = low if s == 0 else ~low
    q_s = jnp.where(pick, q, jnp.zeros_like(q)) * jnp.asarray(SCALE, BF16)
    do_s = jnp.where(pick, do, jnp.zeros_like(do))
    return q_s, do_s


def own_terms(q, do, k, v, lse, delta, low, dq_t, dk, dv):
    kt = k.T * jnp.asarray(SCALE, BF16)
    rows, cols = diagonal()
    mask = rows <= cols
    wide_mask = jnp.concatenate([mask, jnp.ones((HALF, HALF), jnp.bool_)], axis=1)
    k0, k1 = [0.0, 0.0], [0.0, 0.0]
    for s in range(2):
        q_s, do_s = head_inputs(q, do, s, low)
        ls, de = lse[s : s + 1, :], delta[s : s + 1, :]
        kt_s = kt[s * HD : (s + 1) * HD, :]
        a, b, c = attend_back_unit(
            q_s, do_s, k[:HALF], v[:HALF], kt_s[:, :HALF], ls, de, wide_mask
        )
        k0[0] = k0[0] + a
        k0[1] = k0[1] + b
        dq_t[s * HD : (s + 1) * HD, :] = c
        a, b, c = attend_back_unit(
            q_s[HALF:],
            do_s[HALF:],
            k[HALF:],
            v[HALF:],
            kt_s[:, HALF:],
            ls[:, HALF:],
            de[:, HALF:],
            mask,
        )
        k1[0] = k1[0] + a
        k1[1] = k1[1] + b
        dq_t[s * HD : (s + 1) * HD, HALF:] += c
    dk[:HALF, :] = k0[0]
    dk[HALF:, :] = k1[0]
    dv[:HALF, :] = k0[1]
    dv[HALF:, :] = k1[1]


def before_terms(q, do, k, v, lse, delta, low, dq_t):
    kt = k.T * jnp.asarray(SCALE, BF16)
    dk, dv = 0.0, 0.0
    for s in range(2):
        q_s, do_s = head_inputs(q, do, s, low)
        a, b, c = attend_back_unit(
            q_s,
            do_s,
            k,
            v,
            kt[s * HD : (s + 1) * HD, :],
            lse[s : s + 1, :],
            delta[s : s + 1, :],
            None,
        )
        dk = dk + a
        dv = dv + b
        dq_t[s * HD : (s + 1) * HD, :] += c
    return dk, dv


def back_first_kernel(flags, q, do, k, v, kh, vh, lse, delta, dq, dk, dv, terms, dq_t):
    low = lax.broadcasted_iota(jnp.int32, (1, PAIR), 1) < HD
    ls, de = lse[0], delta[0]
    own_terms(q[...], do[...], k[...], v[...], ls, de, low, dq_t, dk, dv)
    wide = flags[0] > 0

    @pl.when(wide)
    def _():
        a, b = before_terms(q[...], do[...], kh[...], vh[...], ls, de, low, dq_t)
        terms[0] = a.astype(BF16)
        terms[1] = b.astype(BF16)

    @pl.when(jnp.logical_not(wide))
    def _():
        terms[...] = jnp.zeros_like(terms)

    dq[...] = dq_t[...].T.astype(BF16)


def back_rest_kernel(
    flags, q, do, k, v, kp, vp, lse, delta, dq0, dk0, dv0, dq, dk, dv, last, dq_t, carry, own
):
    low = lax.broadcasted_iota(jnp.int32, (1, PAIR), 1) < HD
    j = pl.program_id(1)
    blocks = pl.num_programs(1)
    b = blocks - 1 - j

    @pl.when(b > 0)
    def _():
        ls, de = lse[0], delta[0]
        own_terms(q[...], do[...], k[...], v[...], ls, de, low, dq_t, own.at[0], own.at[1])

        @pl.when(j == 0)
        def _():
            last[...] = own[...]

        @pl.when(j > 0)
        def _():
            dk[...] = (own[0] + carry[0]).astype(BF16)
            dv[...] = (own[1] + carry[1]).astype(BF16)

        wide = flags[b] > 0

        @pl.when(wide)
        def _():
            a, bb = before_terms(q[...], do[...], kp[...], vp[...], ls, de, low, dq_t)
            carry[0] = a
            carry[1] = bb

        @pl.when(jnp.logical_not(wide))
        def _():
            carry[...] = jnp.zeros_like(carry)

        dq[...] = dq_t[...].T.astype(BF16)

    @pl.when(b == 0)
    def _():
        dq[...] = dq0[...]
        dk[...] = (dk0[...] + carry[0]).astype(BF16)
        dv[...] = (dv0[...] + carry[1]).astype(BF16)


def last_kernel(
    rows,
    h1,
    dq,
    dk,
    dv,
    last,
    arrived,
    du1,
    z1,
    x,
    gx,
    parts1,
    sums1,
    gain1,
    ln_gain,
    w_qkv,
    w_gate1,
    grad_x,
    g_w,
    sums,
    g_gate1,
    acc,
    st,
    dqkv,
):
    i = pl.program_id(0)
    final = i == pl.num_programs(0) - 1
    count = 1.0 / (rows * parts1.shape[0])
    width = x.shape[1]

    @pl.when(i == 0)
    def _():
        mean, rstd = merge_stats(parts1, rows)
        st[2:3, :] = mean
        st[3:4, :] = rstd
        st[4:5, :] = jnp.sum(sums1[:, 0, :], axis=0, keepdims=True)
        st[5:6, :] = jnp.sum(sums1[:, 1, :], axis=0, keepdims=True)
        g_gate1[0:2, :] = st[4:6, :]
        g_gate1[2:3, :] = jnp.sum(sums1[:, 2, :], axis=0, keepdims=True)
        g_gate1[3:4, :] = jnp.sum(sums1[:, 3, :], axis=0, keepdims=True)
        acc[...] = jnp.zeros_like(acc)

    nhat = (z1[...] - st[2:3, :]) * st[3:4, :]
    dz = (
        (row(gain1) * st[3:4, :]) * (du1[...] - st[4:5, :] * count - nhat * (st[5:6, :] * count))
    ).astype(BF16)
    dqkv[:, :width] = dq[...]

    @pl.when(jnp.logical_not(final))
    def _():
        dqkv[:, width : 2 * width] = dk[...]
        dqkv[:, 2 * width :] = dv[...]

    @pl.when(final)
    def _():
        dqkv[:, width : 2 * width] = (last[0] + arrived[0].astype(F32)).astype(BF16)
        dqkv[:, 2 * width :] = (last[1] + arrived[1].astype(F32)).astype(BF16)

    h = h1[...]
    d = dqkv[...]
    acc[:, : 3 * width] += dot_tn(h, d)
    acc[:, 3 * width :] += dot_tn(h, dz)
    dh = dot_nt(d, w_qkv[...]) + dot_nt(dz, w_gate1[...])
    n, r = normed(x[...].astype(F32))
    e = dh * row(ln_gain)
    grad_x[...] = gx[...] + r * (
        e - jnp.mean(e, axis=-1, keepdims=True) - n * jnp.mean(e * n, axis=-1, keepdims=True)
    )
    add_sums(sums, [column_sum(dh * n), column_sum(dh)], i)

    @pl.when(final)
    def _():
        g_w[...] = acc[...].astype(BF16)


def stage_list():
    out = []
    for axis in AXES:
        bit = 1
        while bit < lax.axis_size(axis):
            out.append((axis, bit))
            bit *= 2
    return out


def swap(x, axis, bit):
    n = lax.axis_size(axis)
    return lax.ppermute(x, axis, [(i, i ^ bit) for i in range(n)])


def upper(axis, bit):
    return (lax.axis_index(axis) & bit) // bit


def sum_everywhere(g):
    stages = stage_list()
    for axis, bit in stages:
        half = g.shape[0] // 2
        mine = upper(axis, bit)
        send = lax.dynamic_slice_in_dim(g, (1 - mine) * half, half, 0)
        keep = lax.dynamic_slice_in_dim(g, mine * half, half, 0)
        got = swap(send, axis, bit)
        g = (keep.astype(F32) + got.astype(F32)).astype(g.dtype)
    for axis, bit in reversed(stages):
        got = swap(g, axis, bit)
        up = upper(axis, bit) > 0
        g = jnp.concatenate([jnp.where(up, got, g), jnp.where(up, g, got)], axis=0)
    return g


def sum_small(v):
    for axis, bit in stage_list():
        v = v + swap(v, axis, bit)
    return v


def continuation(lengths, span):
    place = jnp.arange(lengths.shape[0], dtype=jnp.int32)
    starts = jnp.sum(jnp.where(place[None, :] < place[:, None], lengths[None, :], 0), axis=1)
    begins = place * span
    hit = (starts[None, :] == begins[:, None]) & (lengths[None, :] > 0)
    return 1 - jnp.max(hit.astype(jnp.int32), axis=1)


def body(
    tokens,
    seq_lengths,
    ln1_gain,
    ln1_bias,
    w_qkv,
    w_out,
    w_gate1,
    gate1_gain,
    gate1_shift,
    ln2_gain,
    ln2_bias,
    w_up,
    b_up,
    w_down,
    b_down,
    w_gate2,
    gate2_gain,
    gate2_shift,
    cotangent,
):
    rows, width = tokens.shape
    units = w_up.shape[1]
    ndev = lax.axis_size("seq") * lax.axis_size("head")
    blocks = rows // SPAN
    pairs = width // PAIR
    heads = width // HD
    count = lax.axis_size("head")
    mac = rows * width * width

    tail = tokens[rows - SPAN :]
    before = lax.ppermute(tail, "head", [(i, i + 1) for i in range(count - 1)])
    flags = lax.dynamic_slice_in_dim(
        continuation(seq_lengths[0], SPAN), lax.axis_index("head") * blocks, blocks, 0
    )

    vec = whole((width,))
    stats_shape = (ndev, 2, width)
    h1, qkv, z1, stats1 = pl.pallas_call(
        first_kernel,
        grid=(blocks,),
        in_specs=[rows_of(width), vec, vec, whole(w_qkv.shape), whole(w_gate1.shape)],
        out_specs=[rows_of(width), rows_of(3 * width), rows_of(width), whole(stats_shape)],
        out_shape=[
            struct((rows, width), BF16),
            struct((rows, 3 * width), BF16),
            struct((rows, width), F32),
            struct(stats_shape, F32),
        ],
        scratch_shapes=[pltpu.VMEM((2, width), F32)],
        compiler_params=params(40),
        cost_estimate=cost(8 * mac, rows * width * 14, rows),
        name="first",
    )(tokens, ln1_gain, ln1_bias, w_qkv, w_gate1)
    parts1 = exchange(stats1)

    kv_halo = pl.pallas_call(
        halo_kernel,
        out_shape=struct((SPAN, 2 * width), BF16),
        compiler_params=pltpu.CompilerParams(vmem_limit_bytes=20 * MIB),
        cost_estimate=cost(4 * SPAN * width * width, 4 * MIB, SPAN),
        name="halo",
    )(before, ln1_gain, ln1_bias, w_qkv)

    def tile(f):
        return pl.BlockSpec((SPAN, PAIR), f)

    att, lse = pl.pallas_call(
        attend_kernel,
        grid_spec=pltpu.PrefetchScalarGridSpec(
            num_scalar_prefetch=1,
            grid=(pairs, blocks),
            in_specs=[
                tile(lambda p, b, f: (b, p)),
                tile(lambda p, b, f: (b, pairs + p)),
                tile(lambda p, b, f: (b, 2 * pairs + p)),
                tile(lambda p, b, f: (jnp.maximum(b - 1, 0), pairs + p)),
                tile(lambda p, b, f: (jnp.maximum(b - 1, 0), 2 * pairs + p)),
                tile(lambda p, b, f: (0, p)),
                tile(lambda p, b, f: (0, pairs + p)),
            ],
            out_specs=[
                tile(lambda p, b, f: (b, p)),
                pl.BlockSpec((1, 2, SPAN), lambda p, b, f: (p, 0, b)),
            ],
        ),
        out_shape=[struct((rows, width), BF16), struct((pairs, 2, rows), F32)],
        compiler_params=params(32, 2),
        cost_estimate=cost(10 * heads * SPAN * SPAN * PAIR * 4, 12 * MIB, heads * SPAN * SPAN * 5),
        name="attend",
    )(flags, qkv, qkv, qkv, qkv, qkv, kv_halo, kv_halo)

    y1, h2, z2, stats2 = pl.pallas_call(
        functools.partial(mix_kernel, rows),
        grid=(blocks,),
        in_specs=[rows_of(width), rows_of(width), rows_of(width), whole(stats_shape)]
        + [vec] * 4
        + [whole(w_out.shape), whole(w_gate2.shape)],
        out_specs=[rows_of(width), rows_of(width), rows_of(width), whole(stats_shape)],
        out_shape=[
            struct((rows, width), F32),
            struct((rows, width), BF16),
            struct((rows, width), F32),
            struct(stats_shape, F32),
        ],
        scratch_shapes=[pltpu.VMEM((2, width), F32), pltpu.VMEM((8, width), F32)],
        compiler_params=params(40),
        cost_estimate=cost(4 * mac, rows * width * 18, rows * width),
        name="mix",
    )(att, tokens, z1, parts1, gate1_gain, gate1_shift, ln2_gain, ln2_bias, w_out, w_gate2)
    parts2 = exchange(stats2)

    act, slope, mlp = pl.pallas_call(
        mlp_kernel,
        grid=(blocks,),
        in_specs=[
            rows_of(width),
            whole(w_up.shape),
            whole((units,)),
            whole(w_down.shape),
            vec,
        ],
        out_specs=[rows_of(units), rows_of(units), rows_of(width)],
        out_shape=[
            struct((rows, units), BF16),
            struct((rows, units), BF16),
            struct((rows, width), F32),
        ],
        compiler_params=params(48),
        cost_estimate=cost(4 * rows * width * units, rows * units * 4, rows * units),
        name="mlp",
    )(h2, w_up, b_up, w_down, b_down)

    output, dmlp, sums2 = pl.pallas_call(
        functools.partial(gate2_kernel, rows),
        grid=(blocks,),
        in_specs=[rows_of(width)] * 4 + [whole(stats_shape), vec, vec],
        out_specs=[rows_of(width), rows_of(width), whole(stats_shape)],
        out_shape=[
            struct((rows, width), BF16),
            struct((rows, width), BF16),
            struct(stats_shape, F32),
        ],
        scratch_shapes=[pltpu.VMEM((2, width), F32), pltpu.VMEM((8, width), F32)],
        compiler_params=params(40),
        cost_estimate=cost(rows * width * 20, rows * width * 18, rows * width),
        name="gate2",
    )(mlp, y1, z2, cotangent, parts2, gate2_gain, gate2_shift)
    parts_du2 = exchange(sums2)

    dh2p, g_up, g_down, g_b = pl.pallas_call(
        mlp_back_kernel,
        grid=(blocks,),
        in_specs=[
            rows_of(width),
            rows_of(units),
            rows_of(units),
            rows_of(width),
            whole(w_up.shape),
            whole(w_down.shape),
        ],
        out_specs=[
            rows_of(width),
            whole(w_up.shape),
            whole(w_down.shape),
            whole((2, units)),
        ],
        out_shape=[
            struct((rows, width), F32),
            struct(w_up.shape, BF16),
            struct(w_down.shape, BF16),
            struct((2, units), F32),
        ],
        scratch_shapes=[pltpu.VMEM((width, units), F32), pltpu.VMEM((width, units), F32)],
        compiler_params=params(56),
        cost_estimate=cost(8 * rows * width * units, rows * units * 5),
        name="mlp_back",
    )(dmlp, act, slope, h2, w_up, w_down)

    sums_shape = (ndev, 4, width)
    rows_pair = pl.BlockSpec((pairs, 2, SPAN), lambda i: (0, 0, i))
    gx, du1, datt, delta, g_mid, sums1, g_gate2 = pl.pallas_call(
        functools.partial(middle_kernel, rows),
        grid=(blocks,),
        in_specs=[rows_of(width)] * 9
        + [whole(stats_shape)] * 3
        + [vec] * 5
        + [whole(w_gate2.shape), whole(w_out.shape)],
        out_specs=[
            rows_of(width),
            rows_of(width),
            rows_of(width),
            rows_pair,
            whole((2 * width, width)),
            whole(sums_shape),
            whole((2, width)),
        ],
        out_shape=[
            struct((rows, width), F32),
            struct((rows, width), F32),
            struct((rows, width), BF16),
            struct((pairs, 2, rows), F32),
            struct((2 * width, width), BF16),
            struct(sums_shape, F32),
            struct((2, width), F32),
        ],
        scratch_shapes=[
            pltpu.VMEM((4, width), F32),
            pltpu.VMEM((8, width), F32),
            pltpu.VMEM((width, width), F32),
            pltpu.VMEM((width, width), F32),
        ],
        compiler_params=params(56),
        cost_estimate=cost(10 * mac, rows * width * 38, rows * width * 2),
        name="middle",
    )(
        cotangent,
        mlp,
        y1,
        z2,
        dh2p,
        att,
        tokens,
        z1,
        h2,
        parts2,
        parts_du2,
        parts1,
        gate2_gain,
        gate2_shift,
        gate1_gain,
        gate1_shift,
        ln2_gain,
        w_gate2,
        w_out,
    )
    parts_du1 = exchange(sums1)

    pair_rows = (1, 2, SPAN)
    dq0, dk0, dv0, terms = pl.pallas_call(
        back_first_kernel,
        grid_spec=pltpu.PrefetchScalarGridSpec(
            num_scalar_prefetch=1,
            grid=(pairs,),
            in_specs=[
                tile(lambda p, f: (0, p)),
                tile(lambda p, f: (0, p)),
                tile(lambda p, f: (0, pairs + p)),
                tile(lambda p, f: (0, 2 * pairs + p)),
                tile(lambda p, f: (0, p)),
                tile(lambda p, f: (0, pairs + p)),
                pl.BlockSpec(pair_rows, lambda p, f: (p, 0, 0)),
                pl.BlockSpec(pair_rows, lambda p, f: (p, 0, 0)),
            ],
            out_specs=[
                tile(lambda p, f: (0, p)),
                tile(lambda p, f: (0, p)),
                tile(lambda p, f: (0, p)),
                pl.BlockSpec((2, SPAN, PAIR), lambda p, f: (0, 0, p)),
            ],
            scratch_shapes=[pltpu.VMEM((PAIR, SPAN), F32)],
        ),
        out_shape=[
            struct((SPAN, width), BF16),
            struct((SPAN, width), F32),
            struct((SPAN, width), F32),
            struct((2, SPAN, width), BF16),
        ],
        compiler_params=params(32, 1),
        cost_estimate=cost(
            10 * heads * SPAN * SPAN * PAIR * 2, 8 * MIB, heads * SPAN * SPAN * 2
        ),
        name="attend_back_first",
    )(flags, qkv, datt, qkv, qkv, kv_halo, kv_halo, lse, delta)
    arrived = lax.ppermute(terms, "head", [(i + 1, i) for i in range(count - 1)])

    def at_block(column):
        return tile(lambda p, j, f: (jnp.maximum(blocks - 1 - j, 1), column * pairs + p))

    def at_prev(column):
        return tile(lambda p, j, f: (jnp.maximum(blocks - 2 - j, 0), column * pairs + p))

    def at_first():
        return tile(lambda p, j, f: (0, p))

    def out_block():
        return tile(lambda p, j, f: (blocks - 1 - j, p))

    row_block = pl.BlockSpec(pair_rows, lambda p, j, f: (p, 0, jnp.maximum(blocks - 1 - j, 1)))
    dq, dk, dv, last = pl.pallas_call(
        back_rest_kernel,
        grid_spec=pltpu.PrefetchScalarGridSpec(
            num_scalar_prefetch=1,
            grid=(pairs, blocks),
            in_specs=[
                at_block(0),
                at_block(0),
                at_block(1),
                at_block(2),
                at_prev(1),
                at_prev(2),
                row_block,
                row_block,
                at_first(),
                at_first(),
                at_first(),
            ],
            out_specs=[
                out_block(),
                out_block(),
                out_block(),
                pl.BlockSpec((2, SPAN, PAIR), lambda p, j, f: (0, 0, p)),
            ],
            scratch_shapes=[
                pltpu.VMEM((PAIR, SPAN), F32),
                pltpu.VMEM((2, SPAN, PAIR), F32),
                pltpu.VMEM((2, SPAN, PAIR), F32),
            ],
        ),
        out_shape=[struct((rows, width), BF16)] * 3 + [struct((2, SPAN, width), F32)],
        compiler_params=params(32, 2),
        cost_estimate=cost(
            10 * heads * SPAN * SPAN * PAIR * 6, 20 * MIB, heads * SPAN * SPAN * 4
        ),
        name="attend_back_rest",
    )(flags, qkv, datt, qkv, qkv, qkv, qkv, lse, delta, dq0, dk0, dv0)

    grad_x, g_in, ln1_sums, g_gate1 = pl.pallas_call(
        functools.partial(last_kernel, rows),
        grid=(blocks,),
        in_specs=[rows_of(width)] * 4
        + [whole((2, SPAN, width))] * 2
        + [rows_of(width)] * 4
        + [whole(stats_shape), whole(sums_shape), vec, vec]
        + [whole(w_qkv.shape), whole(w_gate1.shape)],
        out_specs=[
            rows_of(width),
            whole((width, 4 * width)),
            whole((2, width)),
            whole((4, width)),
        ],
        out_shape=[
            struct((rows, width), F32),
            struct((width, 4 * width), BF16),
            struct((2, width), F32),
            struct((4, width), F32),
        ],
        scratch_shapes=[
            pltpu.VMEM((width, 4 * width), F32),
            pltpu.VMEM((8, width), F32),
            pltpu.VMEM((SPAN, 3 * width), BF16),
        ],
        compiler_params=params(56),
        cost_estimate=cost(16 * mac, rows * width * 26),
        name="last",
    )(
        h1,
        dq,
        dk,
        dv,
        last,
        arrived,
        du1,
        z1,
        tokens,
        gx,
        parts1,
        parts_du1,
        gate1_gain,
        ln1_gain,
        w_qkv,
        w_gate1,
    )

    g_down = sum_everywhere(g_down).astype(F32)
    g_up = sum_everywhere(g_up).astype(F32)
    g_mid = sum_everywhere(g_mid).astype(F32)
    g_in = sum_everywhere(g_in).astype(F32)
    g_b = sum_small(g_b)
    ln1_sums = sum_small(ln1_sums)
    return (
        output,
        grad_x,
        ln1_sums[0],
        ln1_sums[1],
        g_in[:, : 3 * width],
        g_mid[width:],
        g_in[:, 3 * width :],
        g_gate1[1],
        g_gate1[0],
        g_gate1[2],
        g_gate1[3],
        g_up,
        g_b[0],
        g_down,
        g_b[1, :width],
        g_mid[:width],
        g_gate2[1],
        g_gate2[0],
    )


def solution(mesh):
    split = P(AXES, None)
    return jax.shard_map(
        body,
        mesh=mesh,
        in_specs=(split, P("seq", None)) + (P(),) * 16 + (split,),
        out_specs=(split, split) + (P(),) * 16,
        check_vma=False,
    )
```

time: 995 us -> 443 us (0.45)
  blocking collectives: 280 us -> 0 us
  matrix products: 211 us -> 0 us
  Pallas kernels: 0 us -> 194 us
  waiting for transfers between devices: 203 us -> 80 us
  local copies, waits for them, and re-layouts: 149 us -> 57.7 us
  starting transfers between devices: 6.58 us -> 82 us
  other arithmetic: 91.5 us -> 19 us
  loops' own time: 27.5 us -> 0 us
  between operations: 15.5 us -> 2.23 us
    psum x7 -> x0, blocking collectives: 280 us -> none  [the longest x2 80.1 us: gate_backward(): lax.psum((jnp.sum(grad_pre, axis=0), jnp.sum(grad_pre * normed, axis=0)),...]
    dot_general x46 -> x0, matrix products: 211 us -> none  [the longest x8 36.2 us: block_scores(): jnp.einsum('qhd,khd->hqk', q_block, k_block, preferred_element_type=jnp.f...]
    pallas_call x0 -> x11, Pallas kernels: none -> 194 us  [the longest x1 38.6 us: body(): pl.pallas_call(back_rest_kernel, grid_spec=pltpu.PrefetchScalarGridSpec(n...]
    psum x1 -> x0, waiting for transfers between devices: 189 us -> none  [body(): lax.psum((g_ln1_gain, g_ln1_bias, g_w_qkv, g_w_out, g_w_gate1, g_w_up, g_...]
    ppermute x2 -> x52, waiting for transfers between devices: 14.5 us -> 79.2 us  [the longest x50 79.2 us: swap(): return lax.ppermute(x, axis, [(i, i ^ bit) for i in range(n)])]
    ppermute x2 -> x52, starting transfers between devices: 6.55 us -> 58.4 us  [the longest x50 51.9 us: swap(): return lax.ppermute(x, axis, [(i, i ^ bit) for i in range(n)])]
    reduce_sum x12 -> x1, other arithmetic: 33.4 us -> 0.11 us  [continuation(): jnp.sum(jnp.where(place[None, :] < place[:, None], lengths[None, :], 0),...]
    dynamic_slice x45 -> x21, local copies, waits for them, and re-layouts: 43.1 us -> 10 us  [the longest x20 9.92 us: sum_everywhere(): send = lax.dynamic_slice_in_dim(g, (1 - mine) * half, half, 0)]
  transfers between devices with their start and end apart: 3 -> 56, of which waited for: 2 -> 31; matrix products, arithmetic and copies ran while one was open for 5% -> 7% of each run, Pallas kernels for 0% -> 35%
where the time goes in v1:
time: 443 us; the launch traced here: 434 us
  Pallas kernels  194 us (44%)
  starting transfers between devices  82 us (19%)
  waiting for transfers between devices  80 us (18%)
  local copies, waits for them, and re-layouts  57.7 us (13%)
  other arithmetic  19 us (4%)
    ppermute x50, waiting for transfers between devices, swap(): return lax.ppermute(x, axis, [(i, i ^ bit) for i in range(n)])  79.2 us
    ppermute x50, starting transfers between devices, swap(): return lax.ppermute(x, axis, [(i, i ^ bit) for i in range(n)])  51.9 us
    unnamed x114, local copies, waits for them, and re-layouts  40.2 us
    pallas_call x1, Pallas kernels, body(): pl.pallas_call(back_rest_kernel, grid_spec=pltpu.PrefetchScalarGridSpec(n...  38.6 us
    pallas_call x1, Pallas kernels, body(): pl.pallas_call(attend_kernel, grid_spec=pltpu.PrefetchScalarGridSpec(num_...  32.4 us
    pallas_call x1, Pallas kernels, body(): pl.pallas_call(mlp_back_kernel, grid=(blocks,), in_specs=[rows_of(width),...  27 us
    all_to_all x4, starting transfers between devices, exchange(): return lax.all_to_all(spread_rows, AXES, 0, 0, tiled=True)  23.6 us
    pallas_call x1, Pallas kernels, body(): pl.pallas_call(functools.partial(middle_kernel, rows), grid=(blocks,), in...  22 us
  transfers between devices with their start and end apart: 56, of which 31 were waited for; matrix products, arithmetic and copies ran while one was open for 7% of the time, Pallas kernels for 35%

profile of v1, /device:TPU:0, one launch (start us, length us, event | category | flops | bytes accessed | tf_op | source)
XLA Modules:
  0.0 434.4 jit_solution(4428262252381204318)
XLA Ops:
  1.7 5.0 %collective-permute-start = (bf16[512,512]{1,0:T(8,128)(2,1)S(1)}, bf16[512,512]{1,0:T(8,128)(2,1)S(1)}, u32[]{:S(2)}, u32[]{:S(2)}) collective-permute-start(bf16[512,512]{1,0:T(8,128)(2,1)S(1)} %slice.45), channel_id=1, source_target_pairs={{0,1},{1,2},{2,3},{4,5},{5,6},{6,7},{8,9},{9,10},{10,11},{12,13},{... | collective-permute-start | bytes 1572872 | tf_op jit(solution)/shard_map/ppermute | solution.py:687
  12.1 8.5 %first.1 = (bf16[2048,512]{1,0:T(8,128)(2,1)S(1)}, bf16[2048,1536]{1,0:T(8,128)(2,1)}, f32[2048,512]{1,0:T(8,128)S(1)}, f32[32,2,512]{2,1,0:T(2,128)}) custom-call(bf16[2048,512]{1,0:T(8,128)(2,1)S(1)} %copy-done.6, f32[512]{0:T(512)S(1)} %copy-done.29, f32[512]{0:T(512)S(1)} %copy-done.27, bf16[512,1536]{1,0:T(8,128)(2,1)S(1)} %copy-done.17, ...), custom_call_target="tpu_custom_call" | custom-call | flops 4294967296 | bytes 14680064 | tf_op jit(solution)/shard_map/first/pallas_call | solution.py:694
  24.0 4.8 %all-to-all-start = ((f32[32,2,512]{2,1,0:T(2,128)}), f32[32,2,512]{2,1,0:T(2,128)S(1)}, u32[]{:S(2)}, u32[]{:S(2)}) async-start(f32[32,2,512]{2,1,0:T(2,128)} %get-tuple-element.60), calls=%async_computation | async-start | bytes 262144 | tf_op jit(solution)/shard_map/all_to_all | solution.py:119
  33.0 32.4 %attend.1 = (bf16[2048,512]{1,0:T(8,128)(2,1)S(1)}, f32[4,2,2048]{2,1,0:T(2,128)S(1)}) custom-call(s32[4]{0:T(128)S(1)} %dynamic_slice.123.flags, bf16[2048,1536]{1,0:T(8,128)(2,1)S(1)} %copy-done, bf16[2048,1536]{1,0:T(8,128)(2,1)S(1)} %copy-done, bf16[2048,1536]{1,0:T(8,128)(2,1)S(1)} %copy-done, bf16[2048,1536]{1,0:T(8,128)(2,1)S(1)} %copy-done, ...), custom_call_target="tpu_custom_call" | custom-call | flops 10737418240 | bytes 12582912 | tf_op jit(solution)/shard_map/attend/pallas_call | solution.py:723
  70.5 8.4 %mix.1 = (f32[2048,512]{1,0:T(8,128)S(1)}, bf16[2048,512]{1,0:T(8,128)(2,1)S(1)}, f32[2048,512]{1,0:T(8,128)}, f32[32,2,512]{2,1,0:T(2,128)}) custom-call(bf16[2048,512]{1,0:T(8,128)(2,1)S(1)} %copy-done.10, bf16[2048,512]{1,0:T(8,128)(2,1)S(1)} %copy-done.7, f32[2048,512]{1,0:T(8,128)} %copy-done.2, f32[32,2,512]{2,1,0:T(2,128)S(1)} %all-to-all-done.parts.parts1, ...), custom_call_target="tpu_custom_call" | custom-call | flops 2147483648 | bytes 18874368 | tf_op jit(solution)/shard_map/mix/pallas_call | solution.py:748
  82.2 4.8 %all-to-all-start.1 = ((f32[32,2,512]{2,1,0:T(2,128)}), f32[32,2,512]{2,1,0:T(2,128)S(1)}, u32[]{:S(2)}, u32[]{:S(2)}) async-start(f32[32,2,512]{2,1,0:T(2,128)} %get-tuple-element.65), calls=%async_computation.1 | async-start | bytes 262144 | tf_op jit(solution)/shard_map/all_to_all | solution.py:119
  90.3 19.2 %mlp.1 = (bf16[2048,2048]{1,0:T(8,128)(2,1)}, bf16[2048,2048]{1,0:T(8,128)(2,1)}, f32[2048,512]{1,0:T(8,128)}) custom-call(bf16[2048,512]{1,0:T(8,128)(2,1)S(1)} %copy-done.14, bf16[512,2048]{1,0:T(8,128)(2,1)S(1)} %copy-done.32, f32[2048]{0:T(1024)S(1)} %copy-done.41, bf16[2048,512]{1,0:T(8,128)(2,1)} %w_down.3, f32[512]{0:T(512)S(1)} %copy-done.42), custom_call_target="tpu_custom_call" | custom-call | flops 8589934592 | bytes 16777216 | tf_op jit(solution)/shard_map/mlp/pallas_call | solution.py:768
  114.0 6.2 %gate2.1 = (bf16[2048,512]{1,0:T(8,128)(2,1)}, bf16[2048,512]{1,0:T(8,128)(2,1)S(1)}, f32[32,2,512]{2,1,0:T(2,128)}) custom-call(f32[2048,512]{1,0:T(8,128)S(1)} %copy-done.5, f32[2048,512]{1,0:T(8,128)S(1)} %copy-done.4, f32[2048,512]{1,0:T(8,128)} %get-tuple-element.64.z2, bf16[2048,512]{1,0:T(8,128)(2,1)S(1)} %copy-done.8, ...), custom_call_target="tpu_custom_call" | custom-call | flops 20971520 | bytes 18874368 | tf_op jit(solution)/shard_map/gate2/pallas_call | solution.py:789
  121.6 27.0 %mlp_back.1 = (f32[2048,512]{1,0:T(8,128)}, bf16[512,2048]{1,0:T(8,128)(2,1)}, bf16[2048,512]{1,0:T(8,128)(2,1)}, f32[2,2048]{1,0:T(2,128)}) custom-call(bf16[2048,512]{1,0:T(8,128)(2,1)} %copy-done.33, bf16[2048,2048]{1,0:T(8,128)(2,1)} %get-tuple-element.69.act, bf16[2048,2048]{1,0:T(8,128)(2,1)} %get-tuple-element.70.slope, bf16[2048,512]{1,0:T(8,128)(2,1)} %copy-done.13, ...), custom_call_target="tpu_custom_call" | custom-call | flops 17179869184 | bytes 20971520 | tf_op jit(solution)/shard_map/mlp_back/pallas_call | solution.py:806
  156.5 4.8 %all-to-all-start.2 = ((f32[32,2,512]{2,1,0:T(2,128)}), f32[32,2,512]{2,1,0:T(2,128)S(1)}, u32[]{:S(2)}, u32[]{:S(2)}) async-start(f32[32,2,512]{2,1,0:T(2,128)} %get-tuple-element.72), calls=%async_computation.2 | async-start | bytes 262144 | tf_op jit(solution)/shard_map/all_to_all | solution.py:119
  165.8 3.4 collective-permute-start.41
  170.6 22.0 %middle.1 = (f32[2048,512]{1,0:T(8,128)}, f32[2048,512]{1,0:T(8,128)}, bf16[2048,512]{1,0:T(8,128)(2,1)}, f32[4,2,2048]{2,1,0:T(2,128)}, bf16[1024,512]{1,0:T(8,...) custom-call(bf16[2048,512]{1,0:T(8,128)(2,1)} %c.3, f32[2048,512]{1,0:T(8,128)} %get-tuple-element.62.mlp, ...), custom_call_target="tpu_custom_call" | custom-call | flops 5368709120 | bytes 39845888 | tf_op jit(solution)/shard_map/middle/pallas_call | solution.py:837
  198.7 9.1 %attend_back_first.1 = (bf16[512,512]{1,0:T(8,128)(2,1)S(1)}, f32[512,512]{1,0:T(8,128)S(1)}, f32[512,512]{1,0:T(8,128)S(1)}, bf16[2,512,512]{2,1,0:T(8,128)(2,1)}) custom-call(s32[4]{0:T(128)S(1)} %dynamic_slice.123.flags, bf16[2048,1536]{1,0:T(8,128)(2,1)S(1)} %bitcast.14, bf16[2048,512]{1,0:T(8,128)(2,1)S(1)} %copy-done.15, ...), custom_call_target="tpu_custom_call" | custom-call | flops 5368709120 | bytes 8388608 | tf_op jit(solution)/shard_map/attend_back_first/pallas_call | solution.py:895
  212.0 9.1 %all-to-all-start.3 = ((f32[32,4,512]{2,1,0:T(4,128)}), f32[32,4,512]{2,1,0:T(4,128)}, u32[]{:S(2)}, u32[]{:S(2)}) async-start(f32[32,4,512]{2,1,0:T(4,128)} %get-tuple-element.86), calls=%async_computation.3 | async-start | bytes 524288 | tf_op jit(solution)/shard_map/all_to_all | solution.py:119
  229.7 38.6 %attend_back_rest.1 = (bf16[2048,512]{1,0:T(8,128)(2,1)S(1)}, bf16[2048,512]{1,0:T(8,128)(2,1)S(1)}, bf16[2048,512]{1,0:T(8,128)(2,1)S(1)}, f32[2,512,512]{2,1,0:T(8,128)S(1)}) custom-call(s32[4]{0:T(128)S(1)} %dynamic_slice.123.flags, bf16[2048,1536]{1,0:T(8,128)(2,1)S(1)} %copy-done.1, bf16[2048,512]{1,0:T(8,128)(2,1)S(1)} %copy-done.16, ...), custom_call_target="tpu_custom_call" | custom-call | flops 16106127360 | bytes 20971520 | tf_op jit(solution)/shard_map/attend_back_rest/pallas_call | solution.py:945
  283.7 21.2 %last.1 = (f32[2048,512]{1,0:T(8,128)}, bf16[512,2048]{1,0:T(8,128)(2,1)}, f32[2,512]{1,0:T(2,128)}, f32[4,512]{1,0:T(4,128)}) custom-call(bf16[2048,512]{1,0:T(8,128)(2,1)} %copy-done.43, bf16[2048,512]{1,0:T(8,128)(2,1)} %copy-done.44, bf16[2048,512]{1,0:T(8,128)(2,1)} %copy-done.45, bf16[2048,512]{1,0:T(8,128)(2,1)} %copy-done.46, ...), custom_call_target="tpu_custom_call" | custom-call | flops 8589934592 | bytes 27262976 | tf_op jit(solution)/shard_map/last/pallas_call | solution.py:983
  324.3 3.6 collective-permute-done.24
  365.5 6.7 %collective-permute-done.8 = bf16[128,2048]{1,0:T(8,128)(2,1)S(1)} collective-permute-done((bf16[128,2048]{1,0:T(8,128)(2,1)S(1)}, bf16[128,2048]{1,0:T(8,128)(2,1)S(1)}, u32[]{:S(2)}, u32[]{:S(2)}) %collective-permute-start.8) | collective-permute-done | bytes 524320 | tf_op jit(solution)/shard_map/ppermute | solution.py:619
  374.1 5.2 %collective-permute-done.9 = bf16[64,2048]{1,0:T(8,128)(2,1)S(1)} collective-permute-done((bf16[64,2048]{1,0:T(8,128)(2,1)S(1)}, bf16[64,2048]{1,0:T(8,128)(2,1)S(1)}, u32[]{:S(2)}, u32[]{:S(2)}) %collective-permute-start.9) | collective-permute-done | bytes 262176 | tf_op jit(solution)/shard_map/ppermute | solution.py:619
  387.1 4.5 %collective-permute-done.11 = bf16[16,2048]{1,0:T(8,128)(2,1)S(1)} collective-permute-done((bf16[16,2048]{1,0:T(8,128)(2,1)S(1)}, bf16[16,2048]{1,0:T(8,128)(2,1)S(1)}, u32[]{:S(2)}, u32[]{:S(2)}) %collective-permute-start.11) | collective-permute-done | bytes 65568 | tf_op jit(solution)/shard_map/ppermute | solution.py:619
  393.5 3.9 collective-permute-done.12
  398.3 4.2 collective-permute-done.13
  409.9 7.7 %collective-permute-done.50 = bf16[512,512]{1,0:T(8,128)(2,1)S(1)} collective-permute-done((bf16[512,512]{1,0:T(8,128)(2,1)S(1)}, bf16[512,512]{1,0:T(8,128)(2,1)S(1)}, u32[]{:S(2)}, u32[]{:S(2)}) %collective-permute-start.50) | collective-permute-done | bytes 524320 | tf_op jit(solution)/shard_map/ppermute | solution.py:619
  418.0 5.3 %collective-permute-done.15 = bf16[128,2048]{1,0:T(8,128)(2,1)S(1)} collective-permute-done((bf16[128,2048]{1,0:T(8,128)(2,1)S(1)}, bf16[128,2048]{1,0:T(8,128)(2,1)S(1)}, u32[]{:S(2)}, u32[]{:S(2)}) %collective-permute-start.15) | collective-permute-done | bytes 524320 | tf_op jit(solution)/shard_map/ppermute | solution.py:619
  (319 shorter events, 166.6 us)
Async XLA Ops:
  1.7 27.5 %collective-permute-start = (bf16[512,512]{1,0:T(8,128)(2,1)S(1)}, bf16[512,512]{1,0:T(8,128)(2,1)S(1)}, u32[]{:S(2)}, u32[]{:S(2)}) collective-permute-start(bf16[512,512]{1,0:T(8,128)(2,1)S(1)} %slice.45), channel_id=1, source_target_pairs={{0,1},{1,2},{2,3},{4,5},{5,6},{6,7},{8,9},{9,10},{10,11},{12,13},{... | collective-permute-start | bytes 1572872 | tf_op jit(solution)/shard_map/ppermute | solution.py:687
  24.0 42.8 %all-to-all-start = ((f32[32,2,512]{2,1,0:T(2,128)}), f32[32,2,512]{2,1,0:T(2,128)S(1)}, u32[]{:S(2)}, u32[]{:S(2)}) async-start(f32[32,2,512]{2,1,0:T(2,128)} %get-tuple-element.60), calls=%async_computation | async-start | bytes 262144 | tf_op jit(solution)/shard_map/all_to_all | solution.py:119
  82.2 27.3 %all-to-all-start.1 = ((f32[32,2,512]{2,1,0:T(2,128)}), f32[32,2,512]{2,1,0:T(2,128)S(1)}, u32[]{:S(2)}, u32[]{:S(2)}) async-start(f32[32,2,512]{2,1,0:T(2,128)} %get-tuple-element.65), calls=%async_computation.1 | async-start | bytes 262144 | tf_op jit(solution)/shard_map/all_to_all | solution.py:119
  156.5 13.4 %all-to-all-start.2 = ((f32[32,2,512]{2,1,0:T(2,128)}), f32[32,2,512]{2,1,0:T(2,128)S(1)}, u32[]{:S(2)}, u32[]{:S(2)}) async-start(f32[32,2,512]{2,1,0:T(2,128)} %get-tuple-element.72), calls=%async_computation.2 | async-start | bytes 262144 | tf_op jit(solution)/shard_map/all_to_all | solution.py:119
  165.7 106.1 %collective-permute-start.27 = (bf16[256,2048]{1,0:T(8,128)(2,1)}, bf16[256,2048]{1,0:T(8,128)(2,1)}, u32[]{:S(2)}, u32[]{:S(2)}) collective-permute-start(bf16[256,2048]{1,0:T(8,128)(2,1)} %constant_dynamic-slice_fusion.9), channel_id=1, source_target_pairs={{0,4},{4,0},{8,12},{12,8},{16,20},{20,16},{24,28},{28,24},{1,5},{5... | collective-permute-start | bytes 3145736 | tf_op jit(solution)/shard_map/ppermute | solution.py:619
  165.8 31.7 %collective-permute-start.41 = (f32[2,2048]{1,0:T(2,128)S(1)}, f32[2,2048]{1,0:T(2,128)S(1)}, u32[]{:S(2)}, u32[]{:S(2)}) collective-permute-start(f32[2,2048]{1,0:T(2,128)S(1)} %add.242), channel_id=1, source_target_pairs={{0,2},{1,3},{2,0},{3,1},{4,6},{5,7},{6,4},{7,5},{8,10},{9,11},{10,... | collective-permute-start | bytes 49160 | tf_op jit(solution)/shard_map/ppermute | solution.py:619
  194.7 26.5 %collective-permute-start.17 = (bf16[512,512]{1,0:T(8,128)(2,1)}, bf16[512,512]{1,0:T(8,128)(2,1)}, u32[]{:S(2)}, u32[]{:S(2)}) collective-permute-start(bf16[512,512]{1,0:T(8,128)(2,1)} %constant_dynamic-slice_fusion.14), channel_id=1, source_target_pairs={{0,4},{4,0},{8,12},{12,8},{16,20},{20,16},{24,28},{28,24},{1,5},{5... | collective-permute-start | bytes 1572872 | tf_op jit(solution)/shard_map/ppermute | solution.py:619
  196.9 78.2 %collective-permute-start.42 = (bf16[1024,512]{1,0:T(8,128)(2,1)}, bf16[1024,512]{1,0:T(8,128)(2,1)}, u32[]{:S(2)}, u32[]{:S(2)}) collective-permute-start(bf16[1024,512]{1,0:T(8,128)(2,1)} %constant_dynamic-slice_fusion.4), channel_id=1, source_target_pairs={{0,4},{4,0},{8,12},{12,8},{16,20},{20,16},{24,28},{28,24},{1,5},{5... | collective-permute-start | bytes 3145736 | tf_op jit(solution)/shard_map/ppermute | solution.py:619
  210.5 73.3 %collective-permute-start.1 = (bf16[2,512,512]{2,1,0:T(8,128)(2,1)}, bf16[2,512,512]{2,1,0:T(8,128)(2,1)}, u32[]{:S(2)}, u32[]{:S(2)}) collective-permute-start(bf16[2,512,512]{2,1,0:T(8,128)(2,1)} %get-tuple-element.83), channel_id=1, source_target_pairs={{1,0},{2,1},{3,2},{5,4},{6,5},{7,6},{9,8},{10,9},{11,10},{13,12},{... | collective-permute-start | bytes 3145736 | tf_op jit(solution)/shard_map/ppermute | solution.py:930
  212.0 71.7 %all-to-all-start.3 = ((f32[32,4,512]{2,1,0:T(4,128)}), f32[32,4,512]{2,1,0:T(4,128)}, u32[]{:S(2)}, u32[]{:S(2)}) async-start(f32[32,4,512]{2,1,0:T(4,128)} %get-tuple-element.86), calls=%async_computation.3 | async-start | bytes 524288 | tf_op jit(solution)/shard_map/all_to_all | solution.py:119
  222.5 49.1 %collective-permute-start.18 = (bf16[256,512]{1,0:T(8,128)(2,1)S(1)}, bf16[256,512]{1,0:T(8,128)(2,1)S(1)}, u32[]{:S(2)}, u32[]{:S(2)}) collective-permute-start(bf16[256,512]{1,0:T(8,128)(2,1)S(1)} %constant_dynamic-slice_fusion.13), channel_id=1, source_target_pairs={{0,8},{4,12},{8,0},{12,4},{16,24},{20,28},{24,16},{28,20},{1,9},{5... | collective-permute-start | bytes 786440 | tf_op jit(solution)/shard_map/ppermute | solution.py:619
  275.1 55.8 %collective-permute-start.28 = (bf16[128,2048]{1,0:T(8,128)(2,1)}, bf16[128,2048]{1,0:T(8,128)(2,1)S(1)}, u32[]{:S(2)}, u32[]{:S(2)}) collective-permute-start(bf16[128,2048]{1,0:T(8,128)(2,1)} %constant_dynamic-slice_fusion.8), channel_id=1, source_target_pairs={{0,8},{4,12},{8,0},{12,4},{16,24},{20,28},{24,16},{28,20},{1,9},{5... | collective-permute-start | bytes 1572872 | tf_op jit(solution)/shard_map/ppermute | solution.py:619
  280.3 52.0 %collective-permute-start.43 = (bf16[512,512]{1,0:T(8,128)(2,1)}, bf16[512,512]{1,0:T(8,128)(2,1)S(1)}, u32[]{:S(2)}, u32[]{:S(2)}) collective-permute-start(bf16[512,512]{1,0:T(8,128)(2,1)} %constant_dynamic-slice_fusion.3), channel_id=1, source_target_pairs={{0,8},{4,12},{8,0},{12,4},{16,24},{20,28},{24,16},{28,20},{1,9},{5... | collective-permute-start | bytes 1572872 | tf_op jit(solution)/shard_map/ppermute | solution.py:619
  281.8 23.2 %collective-permute-start.21 = (bf16[32,512]{1,0:T(8,128)(2,1)S(1)}, bf16[32,512]{1,0:T(8,128)(2,1)S(1)}, u32[]{:S(2)}, u32[]{:S(2)}) collective-permute-start(bf16[32,512]{1,0:T(8,128)(2,1)S(1)} %constant_dynamic-slice_fusion.10), channel_id=1, source_target_pairs={{0,2},{1,3},{2,0},{3,1},{4,6},{5,7},{6,4},{7,5},{8,10},{9,11},{10,... | collective-permute-start | bytes 98312 | tf_op jit(solution)/shard_map/ppermute | solution.py:619
  310.2 51.0 %collective-permute-start.7 = (bf16[256,2048]{1,0:T(8,128)(2,1)S(1)}, bf16[256,2048]{1,0:T(8,128)(2,1)S(1)}, u32[]{:S(2)}, u32[]{:S(2)}) collective-permute-start(bf16[256,2048]{1,0:T(8,128)(2,1)S(1)} %constant_dynamic-slice_fusion.19), channel_id=1, source_target_pairs={{0,4},{4,0},{8,12},{12,8},{16,20},{20,16},{24,28},{28,24},{1,5},{5... | collective-permute-start | bytes 3145736 | tf_op jit(solution)/shard_map/ppermute | solution.py:619
  332.5 7.8 %collective-permute-start.44 = (bf16[256,512]{1,0:T(8,128)(2,1)S(1)}, bf16[256,512]{1,0:T(8,128)(2,1)S(1)}, u32[]{:S(2)}, u32[]{:S(2)}) collective-permute-start(bf16[256,512]{1,0:T(8,128)(2,1)S(1)} %constant_dynamic-slice_fusion.2), channel_id=1, source_target_pairs={{0,16},{4,20},{8,24},{12,28},{16,0},{20,4},{24,8},{28,12},{1,17},{... | collective-permute-start | bytes 786440 | tf_op jit(solution)/shard_map/ppermute | solution.py:619
  335.4 38.2 %collective-permute-start.26 = (bf16[512,512]{1,0:T(8,128)(2,1)S(1)}, bf16[512,512]{1,0:T(8,128)(2,1)S(1)}, u32[]{:S(2)}, u32[]{:S(2)}) collective-permute-start(bf16[512,512]{1,0:T(8,128)(2,1)S(1)} %pad_maximum_fusion.4), channel_id=1, source_target_pairs={{0,4},{4,0},{8,12},{12,8},{16,20},{20,16},{24,28},{28,24},{1,5},{5... | collective-permute-start | bytes 1572872 | tf_op jit(solution)/shard_map/ppermute | solution.py:619
  361.7 10.5 %collective-permute-start.8 = (bf16[128,2048]{1,0:T(8,128)(2,1)S(1)}, bf16[128,2048]{1,0:T(8,128)(2,1)S(1)}, u32[]{:S(2)}, u32[]{:S(2)}) collective-permute-start(bf16[128,2048]{1,0:T(8,128)(2,1)S(1)} %constant_dynamic-slice_fusion.18), channel_id=1, source_target_pairs={{0,8},{4,12},{8,0},{12,4},{16,24},{20,28},{24,16},{28,20},{1,9},{5... | collective-permute-start | bytes 1572872 | tf_op jit(solution)/shard_map/ppermute | solution.py:619
  363.0 24.0 %collective-permute-start.34 = (bf16[64,2048]{1,0:T(8,128)(2,1)S(1)}, bf16[64,2048]{1,0:T(8,128)(2,1)S(1)}, u32[]{:S(2)}, u32[]{:S(2)}) collective-permute-start(bf16[64,2048]{1,0:T(8,128)(2,1)S(1)} %pad_maximum_fusion.9), channel_id=1, source_target_pairs={{0,16},{4,20},{8,24},{12,28},{16,0},{20,4},{24,8},{28,12},{1,17},{... | collective-permute-start | bytes 786440 | tf_op jit(solution)/shard_map/ppermute | solution.py:619
  364.3 33.6 %collective-permute-start.49 = (bf16[256,512]{1,0:T(8,128)(2,1)S(1)}, bf16[256,512]{1,0:T(8,128)(2,1)S(1)}, u32[]{:S(2)}, u32[]{:S(2)}) collective-permute-start(bf16[256,512]{1,0:T(8,128)(2,1)S(1)} %pad_maximum_fusion.10), channel_id=1, source_target_pairs={{0,16},{4,20},{8,24},{12,28},{16,0},{20,4},{24,8},{28,12},{1,17},{... | collective-permute-start | bytes 786440 | tf_op jit(solution)/shard_map/ppermute | solution.py:619
  392.3 14.9 %collective-permute-start.35 = (bf16[128,2048]{1,0:T(8,128)(2,1)S(1)}, bf16[128,2048]{1,0:T(8,128)(2,1)S(1)}, u32[]{:S(2)}, u32[]{:S(2)}) collective-permute-start(bf16[128,2048]{1,0:T(8,128)(2,1)S(1)} %pad_maximum_fusion.5), channel_id=1, source_target_pairs={{0,8},{4,12},{8,0},{12,4},{16,24},{20,28},{24,16},{28,20},{1,9},{5... | collective-permute-start | bytes 1572872 | tf_op jit(solution)/shard_map/ppermute | solution.py:619
  398.1 19.5 %collective-permute-start.50 = (bf16[512,512]{1,0:T(8,128)(2,1)S(1)}, bf16[512,512]{1,0:T(8,128)(2,1)S(1)}, u32[]{:S(2)}, u32[]{:S(2)}) collective-permute-start(bf16[512,512]{1,0:T(8,128)(2,1)S(1)} %pad_maximum_fusion.6), channel_id=1, source_target_pairs={{0,8},{4,12},{8,0},{12,4},{16,24},{20,28},{24,16},{28,20},{1,9},{5... | collective-permute-start | bytes 1572872 | tf_op jit(solution)/shard_map/ppermute | solution.py:619
  409.2 14.1 %collective-permute-start.15 = (bf16[128,2048]{1,0:T(8,128)(2,1)S(1)}, bf16[128,2048]{1,0:T(8,128)(2,1)S(1)}, u32[]{:S(2)}, u32[]{:S(2)}) collective-permute-start(bf16[128,2048]{1,0:T(8,128)(2,1)S(1)} %pad_maximum_fusion.3), channel_id=1, source_target_pairs={{0,8},{4,12},{8,0},{12,4},{16,24},{20,28},{24,16},{28,20},{1,9},{5... | collective-permute-start | bytes 1572872 | tf_op jit(solution)/shard_map/ppermute | solution.py:619
  409.8 13.8 %collective-permute-start.36 = (bf16[256,2048]{1,0:T(8,128)(2,1)S(1)}, bf16[256,2048]{1,0:T(8,128)(2,1)S(1)}, u32[]{:S(2)}, u32[]{:S(2)}) collective-permute-start(bf16[256,2048]{1,0:T(8,128)(2,1)S(1)} %pad_maximum_fusion.1), channel_id=1, source_target_pairs={{0,4},{4,0},{8,12},{12,8},{16,20},{20,16},{24,28},{28,24},{1,5},{5... | collective-permute-start | bytes 3145736 | tf_op jit(solution)/shard_map/ppermute | solution.py:619
  (89 other events, 790.7 us)
